TPU v7x, 32 devices: a whole 2x2x4 slice. The times are simulated.
32 devices in a mesh: blk: 16 (over z, y, core), col: 2 (over x).
Axes of the slice: x: 2, y: 2, z: 4, core: 2. Of those that a mesh axis runs over, the one named last changes fastest.
Arguments:
- node_feats: bfloat16 [256, 32768], P('col', 'blk'), may hold values from -6 to 6
- tile_dst: int32 [896], P('blk'), may hold values from 0 to 15
- tile_src: int32 [896], P('blk'), may hold values from 0 to 47, as said below
- tile_cnt: int32 [896, 128, 128], P('blk'), may hold values from 0 to 3, as said below
- send_blk: int32 [16, 8, 4], P('blk'), may hold values from 0 to 15
- self_weight: bfloat16 [256, 256], replicated, may hold values from -0.375 to 0.375
- neigh_weight: bfloat16 [256, 256], replicated, may hold values from -0.75 to 0.75
- bias: float32 [256], replicated, may hold values from -4 to 4
- cotangent: bfloat16 [256, 32768], P('col', 'blk'), may hold values from -6 to 6
Outputs:
- grad_feats: bfloat16 [256, 32768], P('col', 'blk')
- grad_self: float32 [256, 256], P('col')
- grad_neigh: float32 [256, 256], P('col')
- grad_bias: float32 [256], P('col')
Inputs may be any that keep to these rules, and one draw needn't show every extreme that they name: `tile_src`: of each device's 56 entries, the first 32 are 16 + a permutation of 0 to 32 - 1 (every received slot is read by one tile); the others are own blocks below 16. `tile_cnt`: edge counts; some rows of a tile are empty.
All inputs are finite; a program needn't handle non-finite values.
Results may differ from a plain program's by a relative error of at most 0.006.
Values may be sent and summed in bfloat16 or wider, within the bound.
A program may use at most 64 MiB of HBM per device.

v0:
```python
import jax
import jax.numpy as jnp
from jax import lax
from jax.sharding import PartitionSpec as P


def shifted(block, axis, distance):
    devices = range(lax.axis_size(axis))
    route = [((i - distance) % len(devices), i) for i in devices]
    return lax.ppermute(block, axis, route)


def gelu_slope(pre_act):
    inner = 0.7978845608 * (pre_act + 0.044715 * pre_act * pre_act * pre_act)
    tanh_value = jnp.tanh(inner)
    return 0.5 * (1.0 + tanh_value) + 0.5 * pre_act * (
        1.0 - tanh_value * tanh_value
    ) * 0.7978845608 * (1.0 + 3.0 * 0.044715 * pre_act * pre_act)


def per_device(
    node_feats, tile_dst, tile_src, tile_cnt, send_blk, self_weight, neigh_weight, bias, cotangent
):
    highest = lax.Precision.HIGHEST
    local_dim, local_rows = node_feats.shape
    block_rows = tile_cnt.shape[1]
    own_blocks = local_rows // block_rows
    num_offsets = send_blk.shape[1]
    slot_cap = send_blk.shape[2]
    slot_total = num_offsets * slot_cap
    col_index = lax.axis_index("col")
    first_feat = col_index * local_dim
    feat_blocks = node_feats.reshape(local_dim, own_blocks, block_rows)
    send_table = send_blk[0].reshape(slot_total)
    outgoing = jnp.take(feat_blocks, send_table, axis=1).reshape(
        local_dim, num_offsets, slot_cap, block_rows
    )
    distances = [(index // 2 + 1) * (1 - 2 * (index % 2)) for index in range(num_offsets)]
    arrived = [shifted(outgoing[:, index], "blk", distances[index]) for index in range(num_offsets)]
    received = jnp.stack(arrived, axis=1).reshape(local_dim, slot_total, block_rows)
    source_buffer = jnp.concatenate([feat_blocks, received], axis=1)
    count_half = tile_cnt.astype(jnp.bfloat16)
    picked = jnp.take(source_buffer, tile_src, axis=1)
    products = jnp.einsum("ctj,tij->cti", picked, count_half, preferred_element_type=jnp.float32)
    dest_onehot = (tile_dst[:, None] == jnp.arange(own_blocks, dtype=jnp.int32)[None, :]).astype(
        jnp.float32
    )
    agg_raw = jnp.einsum("cti,tb->cbi", products, dest_onehot, precision=highest)
    degree = jnp.einsum(
        "ti,tb->bi", jnp.sum(tile_cnt, axis=2).astype(jnp.float32), dest_onehot, precision=highest
    )
    floor_degree = jnp.maximum(degree, 1.0)
    aggregate = (agg_raw / floor_degree[None]).astype(jnp.bfloat16).reshape(local_dim, local_rows)
    self_rows = lax.dynamic_slice_in_dim(self_weight, first_feat, local_dim, 0)
    neigh_rows = lax.dynamic_slice_in_dim(neigh_weight, first_feat, local_dim, 0)
    contract_first = (((0,), (0,)), ((), ()))
    self_part = self_rows
    neigh_part = neigh_rows
    pre_act = lax.psum_scatter(
        lax.dot_general(self_part, node_feats, contract_first, preferred_element_type=jnp.float32)
        + lax.dot_general(
            neigh_part, aggregate, contract_first, preferred_element_type=jnp.float32
        ),
        "col",
        scatter_dimension=0,
        tiled=True,
    )
    pre_act = pre_act + lax.dynamic_slice_in_dim(bias, first_feat, local_dim, 0)[:, None]
    grad_pre = (cotangent.astype(jnp.float32) * gelu_slope(pre_act)).astype(jnp.bfloat16)
    contract_last = (((1,), (1,)), ((), ()))
    grad_part = lax.all_gather(grad_pre, "col", axis=0, tiled=True)
    self_part = self_rows
    neigh_part = neigh_rows
    self_acc = jnp.dot(self_part, grad_part, preferred_element_type=jnp.float32)
    neigh_acc = jnp.dot(neigh_part, grad_part, preferred_element_type=jnp.float32)
    self_piece = lax.dot_general(
        node_feats, grad_part, contract_last, preferred_element_type=jnp.float32
    )
    neigh_piece = lax.dot_general(
        aggregate, grad_part, contract_last, preferred_element_type=jnp.float32
    )
    self_grad = self_piece
    neigh_grad = neigh_piece
    self_acc, neigh_acc, self_grad, neigh_grad = (self_acc, neigh_acc, self_grad, neigh_grad)
    bias_local = jnp.sum(grad_pre.astype(jnp.float32), axis=1)
    grad_self, grad_neigh, grad_bias = lax.psum((self_grad, neigh_grad, bias_local), "blk")
    scaled = (neigh_acc.reshape(local_dim, own_blocks, block_rows) / floor_degree[None]).astype(
        jnp.bfloat16
    )
    scaled_tiles = jnp.take(scaled, tile_dst, axis=1)
    contrib = jnp.einsum(
        "cti,tij->ctj", scaled_tiles, count_half, preferred_element_type=jnp.float32
    )
    source_onehot = (
        tile_src[:, None] == jnp.arange(own_blocks + slot_total, dtype=jnp.int32)[None, :]
    ).astype(jnp.float32)
    spread = jnp.einsum("ctj,ts->csj", contrib, source_onehot, precision=highest)
    back_local = spread[:, :own_blocks]
    returning = spread[:, own_blocks:].reshape(local_dim, num_offsets, slot_cap, block_rows)
    back_parts = [
        shifted(returning[:, index], "blk", -distances[index]) for index in range(num_offsets)
    ]
    came_back = jnp.stack(back_parts, axis=1).reshape(local_dim, slot_total, block_rows)
    send_onehot = (send_table[:, None] == jnp.arange(own_blocks, dtype=jnp.int32)[None, :]).astype(
        jnp.float32
    )
    back_remote = jnp.einsum("csj,sb->cbj", came_back, send_onehot, precision=highest)
    grad_feats = (self_acc + (back_local + back_remote).reshape(local_dim, local_rows)).astype(
        jnp.bfloat16
    )
    return (grad_feats, grad_self, grad_neigh, grad_bias)


def solution(mesh):
    placed = (
        P("col", "blk"),
        P("blk"),
        P("blk"),
        P("blk", None, None),
        P("blk", None, None),
        P(),
        P(),
        P(),
        P("col", "blk"),
    )
    return jax.shard_map(
        per_device,
        mesh=mesh,
        in_specs=placed,
        out_specs=(P("col", "blk"), P("col", None), P("col", None), P("col")),
        check_vma=False,
    )
```

profile of v0, /device:TPU:0, one launch (start us, length us, event | category | flops | bytes accessed | tf_op | source)
XLA Modules:
  0.0 268.6 jit_solution(7149439707634592191)
XLA Ops:
  7.2 0.7 compare_and_fusion.1
  7.9 0.8 copy.47
  8.7 0.1 copy.46
  8.8 0.7 compare_select_fusion.3
  9.5 0.1 reshape_squeeze.8
  9.5 1.3 copy.45
  10.9 0.3 copy.49
  11.2 0.7 gather_fusion
  11.9 0.2 broadcast_select_fusion
  12.1 0.9 slice_bitcast_fusion.8
  13.0 5.1 %collective-permute-start.7 = (bf16[128,4,128]{2,0,1:T(8,128)(2,1)S(1)}, bf16[128,4,128]{2,0,1:T(8,128)(2,1)}, u32[]{:S(2)}, u32[]{:S(2)}) collective-permute-start(bf16[128,4,128]{2,0,1:T(8,128)(2,1)S(1)} %get-tuple-element.28), channel_id=1, source_target_pairs={{8,0},{10,2},{12,4},{14,6},{16,8},{18,10},{20,12},{22,14},{24,16},... | collective-permute-start | bytes 393224 | tf_op jit(solution)/shard_map/ppermute | solution.py:10
  18.1 2.7 %collective-permute-start.5 = (bf16[128,4,128]{2,0,1:T(8,128)(2,1)}, bf16[128,4,128]{2,0,1:T(8,128)(2,1)}, u32[]{:S(2)}, u32[]{:S(2)}) collective-permute-start(bf16[128,4,128]{2,0,1:T(8,128)(2,1)} %get-tuple-element.30), channel_id=1, source_target_pairs={{6,0},{8,2},{10,4},{12,6},{14,8},{16,10},{18,12},{20,14},{22,16},{... | collective-permute-start | bytes 393224 | tf_op jit(solution)/shard_map/ppermute | solution.py:10
  20.8 2.2 collective-permute-start
  23.0 3.1 %reduce_sum.18 = s32[56,128]{1,0:T(8,128)S(1)} reduce(s32[56,128,128]{2,1,0:T(8,128)} %param.12, s32[]{:T(128)} %constant.27.clone.1), dimensions={2}, to_apply=%region_0.1 | reduce | flops 910336 | bytes 3698692 | tf_op jit(solution)/shard_map/reduce_sum | solution.py:50
  26.1 0.1 convolution_maximum_fusion
  26.3 0.5 fusion.41
  26.7 0.5 compare_and_fusion.2
  27.3 4.3 %collective-permute-done = bf16[128,4,128]{2,0,1:T(8,128)(2,1)} collective-permute-done((bf16[128,4,128]{2,0,1:T(8,128)(2,1)}, bf16[128,4,128]{2,0,1:T(8,128)(2,1)}, u32[]{:S(2)}, u32[]{:S(2)}) %collective-permute-start) | collective-permute-done | bytes 131104 | tf_op jit(solution)/shard_map/ppermute | solution.py:10
  31.6 0.9 bitcast_dynamic-update-slice_fusion.15
  32.5 1.6 collective-permute-done.1
  34.1 8.6 %collective-permute-done.2 = bf16[128,4,128]{2,0,1:T(8,128)(2,1)S(1)} collective-permute-done((bf16[128,4,128]{2,0,1:T(8,128)(2,1)S(1)}, bf16[128,4,128]{2,0,1:T(8,128)(2,1)S(1)}, u32[]{:S(2)}, u32[]{:S(2)}) %collective-permute-start.2) | collective-permute-done | bytes 131104 | tf_op jit(solution)/shard_map/ppermute | solution.py:10
  42.8 5.1 %collective-permute-done.3 = bf16[128,4,128]{2,0,1:T(8,128)(2,1)S(1)} collective-permute-done((bf16[128,4,128]{2,0,1:T(8,128)(2,1)S(1)}, bf16[128,4,128]{2,0,1:T(8,128)(2,1)S(1)}, u32[]{:S(2)}, u32[]{:S(2)}) %collective-permute-start.3) | collective-permute-done | bytes 131104 | tf_op jit(solution)/shard_map/ppermute | solution.py:10
  47.9 0.9 bitcast_dynamic-update-slice_fusion.11
  48.8 0.9 bitcast_dynamic-update-slice_fusion.10
  49.8 0.9 bitcast_dynamic-update-slice_fusion.9
  50.7 0.9 bitcast_dynamic-update-slice_fusion.8
  51.6 1.3 pad_maximum_fusion
  52.9 3.5 %gather_fusion.1 = bf16[56,128,128]{2,1,0:T(8,128)(2,1)} fusion(bf16[128,48,128]{2,0,1:T(8,128)(2,1)} %pad_maximum_fusion, s32[1024]{0:T(1024)S(1)} %get-tuple-element.36), kind=kCustom, calls=%fused_computation.1 | custom fusion | bytes 3670240 | tf_op jit(solution)/shard_map/jit(_take)/gather | solution.py:43
  56.4 4.0 %convolution_bitcast_fusion.1 = f32[128,56,128]{2,0,1:T(8,128)S(1)} fusion(bf16[56,128,128]{2,1,0:T(8,128)(2,1)} %gather_fusion.1, pred[56]{0:T(512)(128)(4,1)S(1)} %copy-done.18, s32[56,128,128]{2,1,0:T(8,128)} %param.12), kind=kOutput, calls=%fused_computation.11 | convolution fusion | flops 236716032 | bytes 9175096 | tf_op jit(solution)/shard_map/ctj,tij->cti/dot_general | solution.py:44
  60.4 3.4 %fusion.18 = bf16[16,128,128]{2,0,1:T(8,128)(2,1)S(1)} fusion(f32[128,56,128]{2,0,1:T(8,128)S(1)} %convolution_bitcast_fusion.1, f32[16,128]{1,0:T(8,128)S(1)} %convolution_maximum_fusion, s32[56]{0:T(128)S(1)} %copy-done.15), kind=kOutput, calls=%fused_computation.26 | convolution fusion | flops 176685952 | bytes 4202720 | tf_op jit(solution)/shard_map/cti,tb->cbi/dot_general | solution.py:48
  63.9 0.8 copy-done.4
  64.7 1.8 convolution_add_fusion
  66.6 0.6 copy-done.19
  67.2 31.1 %reduce-scatter.2.cloned.1.call-done = f32[128,2048]{1,0:T(8,128)} async-done(((f32[256,2048]{1,0:T(8,128)}), f32[128,2048]{1,0:T(8,128)}) %reduce-scatter.2.cloned.1.call-update) | async-done | bytes 1048592 | tf_op jit(solution)/shard_map/reduce_scatter | solution.py:59
  98.3 2.9 %convert_reduce_fusion = (f32[128]{0:T(128)S(1)}, bf16[128,2048]{1,0:T(8,128)(2,1)}) fusion(f32[128,2048]{1,0:T(8,128)} %reduce-scatter.2.cloned.1.call-done, f32[128]{0:T(128)S(1)} %dynamic_slice.11, bf16[128,2048]{1,0:T(8,128)(2,1)S(1)} %copy-done.6), kind=kLoop, calls=%fused_computation.38 | loop fusion | flops 6029184 | bytes 2098176 | tf_op jit(solution)/shard_map/reduce_sum | solution.py:85
  101.2 0.2 all-reduce.3.cloned.1.call-start
  101.5 21.2 %all-gather.2.cloned.1.call-done = bf16[256,2048]{1,0:T(8,128)(2,1)} async-done(((bf16[128,2048]{1,0:T(8,128)(2,1)}), bf16[256,2048]{1,0:T(8,128)(2,1)}) %all-gather.2.cloned.1.call-update) | async-done | bytes 1048592 | tf_op jit(solution)/shard_map/all_gather | solution.py:71
  122.7 1.5 convolution_bitcast_fusion.3
  124.2 0.1 fusion.28
  124.3 0.9 gather_fusion.2
  125.3 2.7 %convolution_bitcast_fusion = f32[128,56,128]{2,0,1:T(8,128)S(1)} fusion(bf16[56,128,128]{2,1,0:T(8,128)(2,1)S(1)} %gather_fusion.2, pred[56]{0:T(512)(128)(4,1)S(1)} %compare_and_fusion, s32[56,128,128]{2,1,0:T(8,128)} %param.12), kind=kOutput, calls=%fused_computation.10 | convolution fusion | flops 236716032 | bytes 9175096 | tf_op jit(solution)/shard_map/cti,tij->ctj/dot_general | solution.py:91
  128.0 4.2 %fusion.5 = f32[128,48,128]{2,1,0:T(8,128)S(1)} fusion(f32[128,56,128]{2,0,1:T(8,128)S(1)} %convolution_bitcast_fusion, s32[56]{0:T(128)S(1)} %copy-done.17), kind=kOutput, calls=%fused_computation.12 | convolution fusion | flops 528484992 | bytes 6815968 | tf_op jit(solution)/shard_map/ctj,ts->csj/dot_general | solution.py:97
  132.2 0.3 slice.87
  132.5 1.3 copy-done.2
  133.8 1.2 slice_bitcast_fusion
  135.0 3.7 %collective-permute-start.8 = (f32[128,4,128]{2,1,0:T(4,128)}, f32[128,4,128]{2,1,0:T(4,128)}, u32[]{:S(2)}, u32[]{:S(2)}) collective-permute-start(f32[128,4,128]{2,1,0:T(4,128)} %get-tuple-element.26), channel_id=1, source_target_pairs={{2,0},{4,2},{6,4},{8,6},{10,8},{12,10},{14,12},{16,14},{18,16},{20... | collective-permute-start | bytes 786440 | tf_op jit(solution)/shard_map/ppermute | solution.py:10
  138.7 1.1 fusion.33
  139.8 1.1 convolution_bitcast_fusion.4
  141.0 0.1 reshape_squeeze.9
  141.1 34.7 %psum.23 = f32[128]{0:T(128)} all-reduce(f32[128]{0:T(128)S(1)} %get-tuple-element.18), channel_id=1, replica_groups=mesh['blk'=16,'col'=2] {'blk'}, use_global_device_ids=true, to_apply=%region_5.6 | all-reduce | flops 128 | bytes 1024 | tf_op jit(solution)/shard_map/psum | solution.py:86
  175.7 3.6 %collective-permute-start.12 = (f32[128,4,128]{2,1,0:T(4,128)S(1)}, f32[128,4,128]{2,1,0:T(4,128)S(1)}, u32[]{:S(2)}, u32[]{:S(2)}) collective-permute-start(f32[128,4,128]{2,1,0:T(4,128)S(1)} %get-tuple-element.22), channel_id=1, source_target_pairs={{6,0},{8,2},{10,4},{12,6},{14,8},{16,10},{18,12},{20,14},{22,16},{... | collective-permute-start | bytes 786440 | tf_op jit(solution)/shard_map/ppermute | solution.py:10
  179.3 56.6 %all-reduce.3.cloned.1.call-done = (f32[128,256]{0,1:T(8,128)}, f32[128,256]{1,0:T(8,128)}) async-done(((f32[128,256]{0,1:T(8,128)}, f32[128,256]{1,0:T(8,128)}), (f32[128,256]{0,1:T(8,128)}, f32[128,256]{1,0:T(8,128)})) %all-reduce.3.cloned.1.call-update) | async-done | bytes 262160 | tf_op jit(solution)/shard_map/psum | solution.py:86
  235.9 1.7 copy.62
  237.5 3.8 %collective-permute-start.10 = (f32[128,4,128]{2,1,0:T(4,128)S(1)}, f32[128,4,128]{2,1,0:T(4,128)S(1)}, u32[]{:S(2)}, u32[]{:S(2)}) collective-permute-start(f32[128,4,128]{2,1,0:T(4,128)S(1)} %copy-done.7), channel_id=1, source_target_pairs={{4,0},{6,2},{8,4},{10,6},{12,8},{14,10},{16,12},{18,14},{20,16},{2... | collective-permute-start | bytes 786440 | tf_op jit(solution)/shard_map/ppermute | solution.py:10
  241.3 1.0 bitcast_dynamic-update-slice_fusion.7
  242.4 1.0 bitcast_dynamic-update-slice_fusion.6
  243.4 2.9 %collective-permute-done.10 = f32[128,4,128]{2,1,0:T(4,128)S(1)} collective-permute-done((f32[128,4,128]{2,1,0:T(4,128)S(1)}, f32[128,4,128]{2,1,0:T(4,128)S(1)}, u32[]{:S(2)}, u32[]{:S(2)}) %collective-permute-start.10) | collective-permute-done | bytes 262176 | tf_op jit(solution)/shard_map/ppermute | solution.py:10
  246.3 7.1 %collective-permute-start.14 = (f32[128,4,128]{2,1,0:T(4,128)S(1)}, f32[128,4,128]{2,1,0:T(4,128)S(1)}, u32[]{:S(2)}, u32[]{:S(2)}) collective-permute-start(f32[128,4,128]{2,1,0:T(4,128)S(1)} %get-tuple-element.27), channel_id=1, source_target_pairs={{8,0},{10,2},{12,4},{14,6},{16,8},{18,10},{20,12},{22,14},{24,16},... | collective-permute-start | bytes 786440 | tf_op jit(solution)/shard_map/ppermute | solution.py:10
  253.4 0.4 collective-permute-done.11
  254.0 3.3 %collective-permute-done.14 = f32[128,4,128]{2,1,0:T(4,128)S(1)} collective-permute-done((f32[128,4,128]{2,1,0:T(4,128)S(1)}, f32[128,4,128]{2,1,0:T(4,128)S(1)}, u32[]{:S(2)}, u32[]{:S(2)}) %collective-permute-start.14) | collective-permute-done | bytes 262176 | tf_op jit(solution)/shard_map/ppermute | solution.py:10
  257.4 0.6 copy.61
  258.0 2.1 fusion.17
  260.1 1.3 fusion.4
  261.4 0.7 copy.109
  (75 shorter events, 0.8 us)
Async XLA Ops:
  7.2 57.5 %copy-start = (bf16[256,256]{1,0:T(8,128)(2,1)S(1)}, bf16[256,256]{1,0:T(8,128)(2,1)}, u32[]{:S(2)}) copy-start(bf16[256,256]{1,0:T(8,128)(2,1)} %param.15) | copy-start | bytes 393220
  7.2 91.1 %reduce-scatter.2.cloned.1.call-start = ((), (), s32[]{:S(2)}) async-start(), calls=%async_computation.1 | async-start | bytes 3145728 | tf_op jit(solution)/shard_map/reduce_scatter | solution.py:59
  13.0 13.1 %copy-start.14 = (s32[56]{0:T(128)S(1)}, s32[56]{0:T(128)}, u32[]{:S(2)}) copy-start(s32[56]{0:T(128)} %param.10) | copy-start | bytes 676
  13.0 13.2 %copy-start.3 = (bf16[128,2048]{1,0:T(8,128)(2,1)S(1)}, bf16[128,2048]{1,0:T(8,128)(2,1)}, u32[]{:S(2)}) copy-start(bf16[128,2048]{1,0:T(8,128)(2,1)} %param.9) | copy-start | bytes 1572868
  13.0 13.3 %copy-start.8 = (bf16[256,256]{1,0:T(8,128)(2,1)S(1)}, bf16[256,256]{1,0:T(8,128)(2,1)}, u32[]{:S(2)}) copy-start(bf16[256,256]{1,0:T(8,128)(2,1)} %param.14) | copy-start | bytes 393220
  13.0 37.7 %collective-permute-start.7 = (bf16[128,4,128]{2,0,1:T(8,128)(2,1)S(1)}, bf16[128,4,128]{2,0,1:T(8,128)(2,1)}, u32[]{:S(2)}, u32[]{:S(2)}) collective-permute-start(bf16[128,4,128]{2,0,1:T(8,128)(2,1)S(1)} %get-tuple-element.28), channel_id=1, source_target_pairs={{8,0},{10,2},{12,4},{14,6},{16,8},{18,10},{20,12},{22,14},{24,16},... | collective-permute-start | bytes 393224 | tf_op jit(solution)/shard_map/ppermute | solution.py:10
  18.1 31.7 %collective-permute-start.6 = (bf16[128,4,128]{2,0,1:T(8,128)(2,1)}, bf16[128,4,128]{2,0,1:T(8,128)(2,1)}, u32[]{:S(2)}, u32[]{:S(2)}) collective-permute-start(bf16[128,4,128]{2,0,1:T(8,128)(2,1)} %get-tuple-element.29), channel_id=1, source_target_pairs={{24,0},{26,2},{28,4},{30,6},{0,8},{2,10},{4,12},{6,14},{8,16},{10,... | collective-permute-start | bytes 393224 | tf_op jit(solution)/shard_map/ppermute | solution.py:10
  18.1 30.7 %collective-permute-start.5 = (bf16[128,4,128]{2,0,1:T(8,128)(2,1)}, bf16[128,4,128]{2,0,1:T(8,128)(2,1)}, u32[]{:S(2)}, u32[]{:S(2)}) collective-permute-start(bf16[128,4,128]{2,0,1:T(8,128)(2,1)} %get-tuple-element.30), channel_id=1, source_target_pairs={{6,0},{8,2},{10,4},{12,6},{14,8},{16,10},{18,12},{20,14},{22,16},{... | collective-permute-start | bytes 393224 | tf_op jit(solution)/shard_map/ppermute | solution.py:10
  20.8 27.1 %collective-permute-start.4 = (bf16[128,4,128]{2,0,1:T(8,128)(2,1)}, bf16[128,4,128]{2,0,1:T(8,128)(2,1)}, u32[]{:S(2)}, u32[]{:S(2)}) collective-permute-start(bf16[128,4,128]{2,0,1:T(8,128)(2,1)} %get-tuple-element.31), channel_id=1, source_target_pairs={{26,0},{28,2},{30,4},{0,6},{2,8},{4,10},{6,12},{8,14},{10,16},{12,... | collective-permute-start | bytes 393224 | tf_op jit(solution)/shard_map/ppermute | solution.py:10
  20.8 10.7 %collective-permute-start = (bf16[128,4,128]{2,0,1:T(8,128)(2,1)}, bf16[128,4,128]{2,0,1:T(8,128)(2,1)}, u32[]{:S(2)}, u32[]{:S(2)}) collective-permute-start(bf16[128,4,128]{2,0,1:T(8,128)(2,1)} %get-tuple-element.35), channel_id=1, source_target_pairs={{30,0},{0,2},{2,4},{4,6},{6,8},{8,10},{10,12},{12,14},{14,16},{16,... | collective-permute-start | bytes 393224 | tf_op jit(solution)/shard_map/ppermute | solution.py:10
  26.1 0.7 copy-start.16
  26.1 5.5 %copy-start.12 = (bf16[128,4,128]{2,0,1:T(8,128)(2,1)S(1)}, bf16[128,4,128]{2,0,1:T(8,128)(2,1)}, u32[]{:S(2)}) copy-start(bf16[128,4,128]{2,0,1:T(8,128)(2,1)} %get-tuple-element.34) | copy-start | bytes 393220
  26.1 8.0 %copy-start.11 = (bf16[128,4,128]{2,0,1:T(8,128)(2,1)S(1)}, bf16[128,4,128]{2,0,1:T(8,128)(2,1)}, u32[]{:S(2)}) copy-start(bf16[128,4,128]{2,0,1:T(8,128)(2,1)} %get-tuple-element.33) | copy-start | bytes 393220
  26.1 16.6 %copy-start.10 = (bf16[128,4,128]{2,0,1:T(8,128)(2,1)S(1)}, bf16[128,4,128]{2,0,1:T(8,128)(2,1)}, u32[]{:S(2)}) copy-start(bf16[128,4,128]{2,0,1:T(8,128)(2,1)} %get-tuple-element.32) | copy-start | bytes 393220
  31.6 2.5 collective-permute-start.1
  34.1 8.6 %collective-permute-start.2 = (bf16[128,4,128]{2,0,1:T(8,128)(2,1)S(1)}, bf16[128,4,128]{2,0,1:T(8,128)(2,1)S(1)}, u32[]{:S(2)}, u32[]{:S(2)}) collective-permute-start(bf16[128,4,128]{2,0,1:T(8,128)(2,1)S(1)} %copy-done.11), channel_id=1, source_target_pairs={{28,0},{30,2},{0,4},{2,6},{4,8},{6,10},{8,12},{10,14},{12,16},{14,... | collective-permute-start | bytes 393224 | tf_op jit(solution)/shard_map/ppermute | solution.py:10
  42.7 5.2 %collective-permute-start.3 = (bf16[128,4,128]{2,0,1:T(8,128)(2,1)S(1)}, bf16[128,4,128]{2,0,1:T(8,128)(2,1)S(1)}, u32[]{:S(2)}, u32[]{:S(2)}) collective-permute-start(bf16[128,4,128]{2,0,1:T(8,128)(2,1)S(1)} %copy-done.10), channel_id=1, source_target_pairs={{4,0},{6,2},{8,4},{10,6},{12,8},{14,10},{16,12},{18,14},{20,16},{2... | collective-permute-start | bytes 393224 | tf_op jit(solution)/shard_map/ppermute | solution.py:10
  52.9 3.5 %copy-start.18 = (pred[56]{0:T(512)(128)(4,1)S(1)}, pred[56]{0:T(512)(128)(4,1)}, u32[]{:S(2)}) copy-start(pred[56]{0:T(512)(128)(4,1)} %compare_and_fusion.2) | copy-start | bytes 172
  56.4 4.0 %copy-start.15 = (s32[56]{0:T(128)S(1)}, s32[56]{0:T(128)}, u32[]{:S(2)}) copy-start(s32[56]{0:T(128)} %param.10) | copy-start | bytes 676
  63.9 0.8 copy-start.4
  66.5 0.7 copy-start.19
  66.5 31.8 %copy-start.6 = (bf16[128,2048]{1,0:T(8,128)(2,1)S(1)}, bf16[128,2048]{1,0:T(8,128)(2,1)}, u32[]{:S(2)}) copy-start(bf16[128,2048]{1,0:T(8,128)(2,1)} %param.17) | copy-start | bytes 1572868
  66.5 56.2 %all-gather.2.cloned.1.call-start = ((), (), s32[]{:S(2)}) async-start(), calls=%async_computation.2 | async-start | bytes 1572864 | tf_op jit(solution)/shard_map/all_gather | solution.py:71
  101.2 134.7 %all-reduce.3.cloned.1.call-start = ((), (), s32[]{:S(2)}) async-start(), calls=%async_computation.3 | async-start | bytes 524288 | tf_op jit(solution)/shard_map/psum | solution.py:86
  125.2 2.8 %copy-start.17 = (s32[56]{0:T(128)S(1)}, s32[56]{0:T(128)}, u32[]{:S(2)}) copy-start(s32[56]{0:T(128)} %param.11) | copy-start | bytes 676
  132.2 1.6 copy-start.2
  133.8 4.9 %copy-start.1 = (bf16[256,2048]{1,0:T(8,128)(2,1)S(1)}, bf16[256,2048]{1,0:T(8,128)(2,1)}, u32[]{:S(2)}) copy-start(bf16[256,2048]{1,0:T(8,128)(2,1)} %all-gather.2.cloned.1.call-done) | copy-start | bytes 3145732
  133.8 4.9 %copy-start.5 = (bf16[16,128,128]{2,0,1:T(8,128)(2,1)S(1)}, bf16[16,128,128]{2,0,1:T(8,128)(2,1)}, u32[]{:S(2)}) copy-start(bf16[16,128,128]{2,0,1:T(8,128)(2,1)} %copy-done.4) | copy-start | bytes 1572868
  135.0 102.6 %collective-permute-start.8 = (f32[128,4,128]{2,1,0:T(4,128)}, f32[128,4,128]{2,1,0:T(4,128)}, u32[]{:S(2)}, u32[]{:S(2)}) collective-permute-start(f32[128,4,128]{2,1,0:T(4,128)} %get-tuple-element.26), channel_id=1, source_target_pairs={{2,0},{4,2},{6,4},{8,6},{10,8},{12,10},{14,12},{16,14},{18,16},{20... | collective-permute-start | bytes 786440 | tf_op jit(solution)/shard_map/ppermute | solution.py:10
  139.8 97.7 %copy-start.7 = (f32[128,4,128]{2,1,0:T(4,128)S(1)}, f32[128,4,128]{2,1,0:T(4,128)}, u32[]{:S(2)}) copy-start(f32[128,4,128]{2,1,0:T(4,128)} %get-tuple-element.24) | copy-start | bytes 786436
  140.9 101.4 %collective-permute-start.9 = (f32[128,4,128]{2,1,0:T(4,128)}, f32[128,4,128]{2,1,0:T(4,128)}, u32[]{:S(2)}, u32[]{:S(2)}) collective-permute-start(f32[128,4,128]{2,1,0:T(4,128)} %get-tuple-element.25), channel_id=1, source_target_pairs={{30,0},{0,2},{2,4},{4,6},{6,8},{8,10},{10,12},{12,14},{14,16},{16,... | collective-permute-start | bytes 786440 | tf_op jit(solution)/shard_map/ppermute | solution.py:10
  175.7 81.6 %collective-permute-start.15 = (f32[128,4,128]{2,1,0:T(4,128)S(1)}, f32[128,4,128]{2,1,0:T(4,128)S(1)}, u32[]{:S(2)}, u32[]{:S(2)}) collective-permute-start(f32[128,4,128]{2,1,0:T(4,128)S(1)} %get-tuple-element.20), channel_id=1, source_target_pairs={{24,0},{26,2},{28,4},{30,6},{0,8},{2,10},{4,12},{6,14},{8,16},{10,... | collective-permute-start | bytes 786440 | tf_op jit(solution)/shard_map/ppermute | solution.py:10
  175.7 78.2 %collective-permute-start.13 = (f32[128,4,128]{2,1,0:T(4,128)S(1)}, f32[128,4,128]{2,1,0:T(4,128)S(1)}, u32[]{:S(2)}, u32[]{:S(2)}) collective-permute-start(f32[128,4,128]{2,1,0:T(4,128)S(1)} %get-tuple-element.21), channel_id=1, source_target_pairs={{26,0},{28,2},{30,4},{0,6},{2,8},{4,10},{6,12},{8,14},{10,16},{12,... | collective-permute-start | bytes 786440 | tf_op jit(solution)/shard_map/ppermute | solution.py:10
  175.7 78.2 %collective-permute-start.12 = (f32[128,4,128]{2,1,0:T(4,128)S(1)}, f32[128,4,128]{2,1,0:T(4,128)S(1)}, u32[]{:S(2)}, u32[]{:S(2)}) collective-permute-start(f32[128,4,128]{2,1,0:T(4,128)S(1)} %get-tuple-element.22), channel_id=1, source_target_pairs={{6,0},{8,2},{10,4},{12,6},{14,8},{16,10},{18,12},{20,14},{22,16},{... | collective-permute-start | bytes 786440 | tf_op jit(solution)/shard_map/ppermute | solution.py:10
  237.5 8.7 %collective-permute-start.10 = (f32[128,4,128]{2,1,0:T(4,128)S(1)}, f32[128,4,128]{2,1,0:T(4,128)S(1)}, u32[]{:S(2)}, u32[]{:S(2)}) collective-permute-start(f32[128,4,128]{2,1,0:T(4,128)S(1)} %copy-done.7), channel_id=1, source_target_pairs={{4,0},{6,2},{8,4},{10,6},{12,8},{14,10},{16,12},{18,14},{20,16},{2... | collective-permute-start | bytes 786440 | tf_op jit(solution)/shard_map/ppermute | solution.py:10
  242.3 11.5 %collective-permute-start.11 = (f32[128,4,128]{2,1,0:T(4,128)S(1)}, f32[128,4,128]{2,1,0:T(4,128)S(1)}, u32[]{:S(2)}, u32[]{:S(2)}) collective-permute-start(f32[128,4,128]{2,1,0:T(4,128)S(1)} %get-tuple-element.23), channel_id=1, source_target_pairs={{28,0},{30,2},{0,4},{2,6},{4,8},{6,10},{8,12},{10,14},{12,16},{14,... | collective-permute-start | bytes 786440 | tf_op jit(solution)/shard_map/ppermute | solution.py:10
  246.3 11.0 %collective-permute-start.14 = (f32[128,4,128]{2,1,0:T(4,128)S(1)}, f32[128,4,128]{2,1,0:T(4,128)S(1)}, u32[]{:S(2)}, u32[]{:S(2)}) collective-permute-start(f32[128,4,128]{2,1,0:T(4,128)S(1)} %get-tuple-element.27), channel_id=1, source_target_pairs={{8,0},{10,2},{12,4},{14,6},{16,8},{18,10},{20,12},{22,14},{24,16},... | collective-permute-start | bytes 786440 | tf_op jit(solution)/shard_map/ppermute | solution.py:10
  258.0 2.2 copy-start.9
  260.1 1.3 copy-start.13
Sparse Core Ops, SparseCore 0:
  66.6 31.6 reduce-scatter.1
  101.3 21.2 all-gather.1
  141.0 94.7 all-reduce.2
where the time goes:
time: 269 us
  waiting for transfers between devices  135 us (50%)
  blocking collectives  34.7 us (13%)
  starting transfers between devices  28.6 us (11%)
  matrix products  23.9 us (9%)
  local copies, waits for them, and re-layouts  22.7 us (8%)
  between operations  14.2 us (5%)
  other arithmetic  9.44 us (4%)
    psum x1, waiting for transfers between devices, per_device(): lax.psum((self_grad, neigh_grad, bias_local), 'blk')  56.6 us
    psum x1, blocking collectives, per_device(): lax.psum((self_grad, neigh_grad, bias_local), 'blk')  34.7 us
    reduce_scatter x1, waiting for transfers between devices, per_device(): lax.psum_scatter(lax.dot_general(self_part, node_feats, contract_first, p...  31.1 us
    ppermute x16, starting transfers between devices, shifted(): return lax.ppermute(block, axis, route)  28.3 us
    ppermute x16, waiting for transfers between devices, shifted(): return lax.ppermute(block, axis, route)  26.2 us
    all_gather x1, waiting for transfers between devices, per_device(): grad_part = lax.all_gather(grad_pre, 'col', axis=0, tiled=True)  21.2 us
    unnamed x58, local copies, waits for them, and re-layouts  13.1 us
  transfers between devices with their start and end apart: 19, of which 10 were waited for; matrix products, arithmetic and copies ran while one was open for 5% of the time, Pallas kernels for 0%

commit v1 on v0

v1 whole, which is shorter than its diff:
```python
import functools

import jax
import jax.numpy as jnp
from jax import lax
from jax.experimental import pallas as pl
from jax.experimental.pallas import tpu as pltpu
from jax.sharding import PartitionSpec as P

MESH = pl.DeviceIdType.MESH
VMEM_BYTES = 40 * 1024 * 1024
STEP_TILES = 8


def gelu_slope(pre_act):
    inner = 0.7978845608 * (pre_act + 0.044715 * pre_act * pre_act * pre_act)
    tanh_value = jnp.tanh(inner)
    return 0.5 * (1.0 + tanh_value) + 0.5 * pre_act * (
        1.0 - tanh_value * tanh_value
    ) * 0.7978845608 * (1.0 + 3.0 * 0.044715 * pre_act * pre_act)


def hop(index):
    return (index // 2 + 1) * (1 - 2 * (index % 2))


def vmem():
    return pl.BlockSpec(memory_space=pltpu.VMEM)


def smem():
    return pl.BlockSpec(memory_space=pltpu.SMEM)


def anywhere():
    return pl.BlockSpec(memory_space=pl.ANY)


def params(collective=None):
    if collective is None:
        return pltpu.CompilerParams(vmem_limit_bytes=VMEM_BYTES)
    return pltpu.CompilerParams(
        vmem_limit_bytes=VMEM_BYTES, collective_id=collective, has_side_effects=True
    )


def positions(num_blk, num_col):
    row, col = lax.axis_index("blk"), lax.axis_index("col")
    col_peer = [(row, lax.rem(col + step, num_col)) for step in range(1, num_col)]
    return row, col, col_peer


def greet(peers):
    barrier = pltpu.get_barrier_semaphore()
    for peer in peers:
        pl.semaphore_signal(barrier, inc=1, device_id=peer, device_id_type=MESH)
    pl.semaphore_wait(barrier, len(peers))


def push(src, dst, send_sem, recv_sem, peer):
    copy = pltpu.make_async_remote_copy(
        src_ref=src,
        dst_ref=dst,
        send_sem=send_sem,
        recv_sem=recv_sem,
        device_id=peer,
        device_id_type=MESH,
    )
    copy.start()
    return copy


def halo_peers(row, col, num_blk, num_hops, sign):
    return [
        (lax.rem(row + sign * hop(index) + num_blk, num_blk), col) for index in range(num_hops)
    ]


def pack_kernel(send_ref, feat_ref, out_ref):
    num_hops, _, width = out_ref.shape
    cap = send_ref.shape[2]
    side = width // cap
    for index in range(num_hops):
        for slot in range(cap):
            start = pl.multiple_of(send_ref[0, index, slot] * side, side)
            out_ref[index, :, slot * side : (slot + 1) * side] = feat_ref[:, pl.ds(start, side)]


def halo_kernel(
    num_blk, num_col, sbuf, feat_ref, cot_ref, recv_ref, feat_all, cot_all,
    halo_send, halo_recv, col_send, col_recv, own_sem,
):
    num_hops = sbuf.shape[0]
    part = feat_all.shape[2]
    row, col, col_peer = positions(num_blk, num_col)
    halo = halo_peers(row, col, num_blk, num_hops, 1)
    greet(halo + col_peer)
    copies = []
    for index in range(num_hops):
        copies.append(
            push(sbuf.at[index], recv_ref.at[index], halo_send.at[index], halo_recv.at[index], halo[index])
        )
    mine = pl.ds(pl.multiple_of(col * part, part), part)
    for at, (source, target) in enumerate(((feat_ref, feat_all), (cot_ref, cot_all))):
        for step, peer in enumerate(col_peer):
            theirs = pl.ds(pl.multiple_of(peer[1] * part, part), part)
            copies.append(
                push(
                    source.at[:, theirs], target.at[col], col_send.at[at, step],
                    col_recv.at[at, step], peer,
                )
            )
        own = pltpu.make_async_copy(source.at[:, mine], target.at[col], own_sem.at[at])
        own.start()
        copies.append(own)
    for copy in copies:
        copy.wait()


def aggregate_kernel(slots, dst_ref, src_ref, feat_ref, recv_ref, cnt_ref, agg_ref, floor_ref, acc):
    step = pl.program_id(0)
    blocks, rows, side = acc.shape
    dim = feat_ref.shape[0]
    num_hops = recv_ref.shape[0]
    cap = slots // num_hops
    tiles = cnt_ref.shape[0]

    @pl.when(step == 0)
    def _():
        acc[...] = jnp.zeros_like(acc)

    def add(tile, picked):
        counts = cnt_ref[tile].astype(jnp.float32).astype(jnp.bfloat16)
        left = jnp.concatenate([picked, jnp.ones((rows - dim, side), jnp.bfloat16)], axis=0)
        product = lax.dot_general(
            left, counts, (((1,), (1,)), ((), ())), preferred_element_type=jnp.float32
        )
        dst = dst_ref[step * tiles + tile]
        acc[dst] += product

    @pl.when(step * tiles < slots)
    def _():
        for tile in range(tiles):
            slot = src_ref[step * tiles + tile] - blocks
            start = pl.multiple_of(lax.rem(slot, cap) * side, side)
            add(tile, recv_ref[lax.div(slot, cap), :, pl.ds(start, side)])

    @pl.when(step * tiles >= slots)
    def _():
        for tile in range(tiles):
            start = pl.multiple_of(src_ref[step * tiles + tile] * side, side)
            add(tile, feat_ref[:, pl.ds(start, side)])

    @pl.when(step == pl.num_programs(0) - 1)
    def _():
        per_part = agg_ref.shape[2] // side
        for block in range(blocks):
            part, at = block // per_part, (block % per_part) * side
            floor = jnp.maximum(acc[block, dim : dim + 1, :], 1.0)
            floor_ref[part, :, at : at + side] = floor
            agg_ref[part, :, at : at + side] = (acc[block, :dim, :] / floor).astype(jnp.bfloat16)


def swap_kernel(num_blk, num_col, src_ref, dst_ref, send_sem, recv_sem, own_sem):
    row, col, col_peer = positions(num_blk, num_col)
    greet(col_peer)
    copies = [
        push(src_ref.at[peer[1]], dst_ref.at[col], send_sem.at[step], recv_sem.at[step], peer)
        for step, peer in enumerate(col_peer)
    ]
    own = pltpu.make_async_copy(src_ref.at[col], dst_ref.at[col], own_sem)
    own.start()
    for copy in copies:
        copy.wait()
    own.wait()


def dense_kernel(
    chunk, feat_ref, agg_ref, cot_ref, floor_ref, ws_ref, wn_ref, bias_ref,
    scaled_ref, self_ref, grad_ref, acc,
):
    width, nodes = feat_ref.shape
    parts, dim, _ = scaled_ref.shape
    col = lax.axis_index("col")
    self_weight, neigh_weight = ws_ref[...], wn_ref[...]
    first = (((0,), (0,)), ((), ()))
    last = (((1,), (1,)), ((), ()))
    bias = bias_ref[...]
    for start in range(0, nodes, chunk):
        at = slice(start, start + chunk)
        feat, agg = feat_ref[:, at], agg_ref[:, at]
        pre_act = (
            lax.dot_general(self_weight, feat, first, preferred_element_type=jnp.float32)
            + lax.dot_general(neigh_weight, agg, first, preferred_element_type=jnp.float32)
            + bias
        )
        dz = (cot_ref[:, at].astype(jnp.float32) * gelu_slope(pre_act)).astype(jnp.bfloat16)
        floor = floor_ref[col, :, at]
        neigh = jnp.dot(neigh_weight, dz, preferred_element_type=jnp.float32) / floor
        own = jnp.dot(self_weight, dz, preferred_element_type=jnp.float32)
        for part in range(parts):
            rows = slice(part * dim, (part + 1) * dim)
            scaled_ref[part, :, at] = neigh[rows].astype(jnp.bfloat16)
            self_ref[part, :, at] = own[rows].astype(jnp.bfloat16)
        ones = jnp.ones((16, chunk), jnp.bfloat16)
        left = jnp.concatenate([feat, agg, ones], axis=0)
        grads = lax.dot_general(left, dz, last, preferred_element_type=jnp.float32)
        if start == 0:
            acc[...] = grads
        else:
            acc[...] += grads
    for part in range(parts):
        rows = slice(part * dim, (part + 1) * dim)
        grad_ref[part, :dim, :width] = acc[rows, :].astype(jnp.bfloat16)
        grad_ref[part, dim:, :width] = acc[width + part * dim : width + (part + 1) * dim, :].astype(
            jnp.bfloat16
        )
        bias_row = acc[2 * width : 2 * width + 1, rows].astype(jnp.bfloat16)
        grad_ref[part, :, width : width + dim] = jnp.broadcast_to(bias_row, (2 * dim, dim))
        if dim < grad_ref.shape[2] - width:
            rest = grad_ref.shape[2] - width - dim
            grad_ref[part, :, width + dim :] = jnp.zeros((2 * dim, rest), jnp.bfloat16)


def spread_kernel(slots, dst_ref, src_ref, scaled_ref, cnt_ref, ret_ref, back_ref):
    step = pl.program_id(0)
    num_hops, _, width = ret_ref.shape
    cap = slots // num_hops
    side = width // cap
    blocks = back_ref.shape[0]
    per_part = scaled_ref.shape[2] // side
    tiles = cnt_ref.shape[0]

    @pl.when(step == 0)
    def _():
        back_ref[...] = jnp.zeros_like(back_ref)

    def contribution(tile):
        dst = dst_ref[step * tiles + tile]
        start = pl.multiple_of(lax.rem(dst, per_part) * side, side)
        picked = scaled_ref[lax.div(dst, per_part), :, pl.ds(start, side)]
        counts = cnt_ref[tile].astype(jnp.float32).astype(jnp.bfloat16)
        return jnp.dot(picked, counts, preferred_element_type=jnp.float32)

    @pl.when(step * tiles < slots)
    def _():
        for tile in range(tiles):
            slot = src_ref[step * tiles + tile] - blocks
            start = pl.multiple_of(lax.rem(slot, cap) * side, side)
            ret_ref[lax.div(slot, cap), :, pl.ds(start, side)] = contribution(tile).astype(
                jnp.bfloat16
            )

    @pl.when(step * tiles >= slots)
    def _():
        for tile in range(tiles):
            back_ref[src_ref[step * tiles + tile]] += contribution(tile)


def return_kernel(
    num_blk, num_col, ret_ref, self_ref, grad_ref, came_ref, self_all, grad_out, bias_out,
    col_buf, rs_src, rs_buf, piece,
    halo_send, halo_recv, col_send, col_recv, rs_send, rs_recv, ag_send, ag_recv, own_sem,
):
    num_hops = ret_ref.shape[0]
    row, col, col_peer = positions(num_blk, num_col)
    width = piece.shape[1]
    halo = halo_peers(row, col, num_blk, num_hops, -1)
    ring = [(lax.rem(row + step, num_blk), col) for step in range(1, num_blk)]
    greet(ring + col_peer)
    first = [
        push(grad_ref.at[peer[1]], col_buf.at[step], col_send.at[0, step], col_recv.at[0, step], peer)
        for step, peer in enumerate(col_peer)
    ]
    later = [
        push(ret_ref.at[index], came_ref.at[index], halo_send.at[index], halo_recv.at[index], halo[index])
        for index in range(num_hops)
    ]
    later += [
        push(self_ref.at[peer[1]], self_all.at[col], col_send.at[1, step], col_recv.at[1, step], peer)
        for step, peer in enumerate(col_peer)
    ]
    own = pltpu.make_async_copy(self_ref.at[col], self_all.at[col], own_sem)
    own.start()
    for copy in first:
        copy.wait()
    for index in range(num_blk):
        total = grad_ref[col, index].astype(jnp.float32)
        for step in range(num_col - 1):
            total += col_buf[step, index].astype(jnp.float32)
        rs_src[index] = total.astype(jnp.bfloat16)
    scatter = [
        push(rs_src.at[peer[0]], rs_buf.at[step], rs_send.at[step], rs_recv.at[step], peer)
        for step, peer in enumerate(ring)
    ]
    total = rs_src[row].astype(jnp.float32)
    for step, copy in enumerate(scatter):
        copy.wait()
        total += rs_buf[step].astype(jnp.float32)
    bias_out[...] = total[0:1, width:]
    piece[...] = total[:, :width].astype(jnp.bfloat16)
    grad_out[row] = piece[...]
    gather = [
        push(piece, grad_out.at[row], ag_send.at[step], ag_recv.at[step], peer)
        for step, peer in enumerate(ring)
    ]
    for copy in gather + later:
        copy.wait()
    own.wait()


def finish_kernel(send_ref, self_ref, back_ref, came_ref, out_ref, acc):
    blocks, _, side = acc.shape
    num_hops, _, width = came_ref.shape
    cap = width // side
    acc[...] = back_ref[...]
    for index in range(num_hops):
        for slot in range(cap):
            came = came_ref[index, :, slot * side : (slot + 1) * side]
            acc[send_ref[0, index, slot]] += came.astype(jnp.float32)
    per_part = self_ref.shape[2] // side
    for block in range(blocks):
        at = (block % per_part) * side
        own = self_ref[block // per_part, :, at : at + side].astype(jnp.float32)
        out_ref[:, block * side : (block + 1) * side] = (acc[block] + own).astype(jnp.bfloat16)


def per_device(
    num_blk, num_col,
    node_feats, tile_dst, tile_src, tile_cnt, send_blk, self_weight, neigh_weight, bias, cotangent,
):
    half, full = jnp.bfloat16, jnp.float32
    dim, rows = node_feats.shape
    tiles, side, _ = tile_cnt.shape
    blocks = rows // side
    num_hops, cap = send_blk.shape[1:]
    slots = num_hops * cap
    part = rows // num_col
    width = self_weight.shape[0]
    dma = pltpu.SemaphoreType.DMA
    shape = jax.ShapeDtypeStruct
    peers = max(num_col - 1, 1)
    split = shape((num_col, dim, part), half)
    slot_shape = shape((num_hops, dim, cap * side), half)

    outgoing = pl.pallas_call(
        pack_kernel,
        out_shape=slot_shape,
        in_specs=[smem(), vmem()],
        out_specs=vmem(),
        compiler_params=params(),
        name="pack",
    )(send_blk, node_feats)
    received, feat_all, cot_all = pl.pallas_call(
        functools.partial(halo_kernel, num_blk, num_col),
        out_shape=(slot_shape, split, split),
        in_specs=[anywhere()] * 3,
        out_specs=(anywhere(),) * 3,
        scratch_shapes=[
            dma((num_hops,)), dma((num_hops,)), dma((2, peers)), dma((2, peers)), dma((2,)),
        ],
        compiler_params=params(0),
        name="halo",
    )(outgoing, node_feats, cotangent)

    steps = tiles // STEP_TILES
    cnt_spec = pl.BlockSpec((STEP_TILES, side, side), lambda step: (step, 0, 0))
    whole = lambda dims: pl.BlockSpec(dims, lambda step: (0,) * len(dims))
    aggregate, floor = pl.pallas_call(
        functools.partial(aggregate_kernel, slots),
        grid=(steps,),
        out_shape=(split, shape((num_col, 1, part), full)),
        in_specs=[smem(), smem(), whole((dim, rows)), whole(slot_shape.shape), cnt_spec],
        out_specs=(whole(split.shape), whole((num_col, 1, part))),
        scratch_shapes=[pltpu.VMEM((blocks, dim + 16, side), full)],
        compiler_params=params(),
        name="aggregate",
    )(tile_dst, tile_src, node_feats, received, tile_cnt)

    def swap(array, collective, name):
        return pl.pallas_call(
            functools.partial(swap_kernel, num_blk, num_col),
            out_shape=split,
            in_specs=[anywhere()],
            out_specs=anywhere(),
            scratch_shapes=[dma((peers,)), dma((peers,)), dma(())],
            compiler_params=params(collective),
            name=name,
        )(array)

    agg_all = swap(aggregate, 1, "swap_aggregate")
    lanes = width + 128
    scaled, own_part, grads = pl.pallas_call(
        functools.partial(dense_kernel, min(part, 256)),
        out_shape=(split, split, shape((num_col, 2 * dim, lanes), half)),
        in_specs=[vmem()] * 7,
        out_specs=(vmem(),) * 3,
        scratch_shapes=[pltpu.VMEM((2 * width + 16, width), full)],
        compiler_params=params(),
        name="dense",
    )(
        feat_all.reshape(width, part), agg_all.reshape(width, part), cot_all.reshape(width, part),
        floor, self_weight, neigh_weight, bias.reshape(width, 1),
    )
    scaled_all = swap(scaled, 2, "swap_scaled")
    returning, back_local = pl.pallas_call(
        functools.partial(spread_kernel, slots),
        grid=(steps,),
        out_shape=(slot_shape, shape((blocks, dim, side), full)),
        in_specs=[smem(), smem(), whole(split.shape), cnt_spec],
        out_specs=(whole(slot_shape.shape), whole((blocks, dim, side))),
        compiler_params=params(),
        name="spread",
    )(tile_dst, tile_src, scaled_all, tile_cnt)

    span = 2 * dim // num_blk
    ring = num_blk - 1
    came, own_all, grad_sum, bias_sum = pl.pallas_call(
        functools.partial(return_kernel, num_blk, num_col),
        out_shape=(slot_shape, split, shape((num_blk, span, width), half), shape((1, 128), full)),
        in_specs=[anywhere(), anywhere(), vmem()],
        out_specs=(anywhere(), anywhere(), vmem(), vmem()),
        scratch_shapes=[
            pltpu.VMEM((peers, num_blk, span, lanes), half),
            pltpu.VMEM((num_blk, span, lanes), half),
            pltpu.VMEM((ring, span, lanes), half),
            pltpu.VMEM((span, width), half),
            dma((num_hops,)), dma((num_hops,)), dma((2, peers)), dma((2, peers)),
            dma((ring,)), dma((ring,)), dma((ring,)), dma((ring,)), dma(()),
        ],
        compiler_params=params(3),
        name="give_back",
    )(returning, own_part, grads.reshape(num_col, num_blk, span, lanes))

    grad_feats = pl.pallas_call(
        finish_kernel,
        out_shape=shape((dim, rows), half),
        in_specs=[smem(), vmem(), vmem(), vmem()],
        out_specs=vmem(),
        scratch_shapes=[pltpu.VMEM((blocks, dim, side), full)],
        compiler_params=params(),
        name="finish",
    )(send_blk, own_all, back_local, came)
    grad_both = grad_sum.reshape(2 * dim, width).astype(full)
    return (grad_feats, grad_both[:dim], grad_both[dim:], bias_sum[0, :dim])


def solution(mesh):
    placed = (
        P("col", "blk"),
        P("blk"),
        P("blk"),
        P("blk", None, None),
        P("blk", None, None),
        P(),
        P(),
        P(),
        P("col", "blk"),
    )
    return jax.shard_map(
        functools.partial(per_device, mesh.shape["blk"], mesh.shape["col"]),
        mesh=mesh,
        in_specs=placed,
        out_specs=(P("col", "blk"), P("col", None), P("col", None), P("col")),
        check_vma=False,
    )
```

time: 269 us -> 83.7 us (0.31)
  waiting for transfers between devices: 135 us -> 0 us
  Pallas kernels: 0 us -> 76.4 us
  blocking collectives: 34.7 us -> 0 us
  starting transfers between devices: 28.6 us -> 0 us
  matrix products: 23.9 us -> 0 us
  local copies, waits for them, and re-layouts: 22.7 us -> 6.17 us
  between operations: 14.2 us -> 0.79 us
  other arithmetic: 9.44 us -> 0 us
    pallas_call x0 -> x9, Pallas kernels: none -> 76.4 us  [the longest x1 29.8 us: per_device(): pl.pallas_call(functools.partial(return_kernel, num_blk, num_col), out_sh...]
    psum x1 -> x0, waiting for transfers between devices: 56.6 us -> none  [per_device(): lax.psum((self_grad, neigh_grad, bias_local), 'blk')]
    psum x1 -> x0, blocking collectives: 34.7 us -> none  [per_device(): lax.psum((self_grad, neigh_grad, bias_local), 'blk')]
    reduce_scatter x1 -> x0, waiting for transfers between devices: 31.1 us -> none  [per_device(): lax.psum_scatter(lax.dot_general(self_part, node_feats, contract_first, p...]
    ppermute x16 -> x0, starting transfers between devices: 28.3 us -> none  [shifted(): return lax.ppermute(block, axis, route)]
    ppermute x16 -> x0, waiting for transfers between devices: 26.2 us -> none  [shifted(): return lax.ppermute(block, axis, route)]
    dot_general x12 -> x0, matrix products: 23.9 us -> none  [the longest x1 4.16 us: per_device(): jnp.einsum('ctj,ts->csj', contrib, source_onehot, precision=highest)]
    all_gather x1 -> x0, waiting for transfers between devices: 21.2 us -> none  [per_device(): grad_part = lax.all_gather(grad_pre, 'col', axis=0, tiled=True)]
  transfers between devices with their start and end apart: 19 -> 0, of which waited for: 10 -> 0; matrix products, arithmetic and copies ran while one was open for 5% -> 0% of each run, Pallas kernels for 0% -> 0%
where the time goes in v1:
time: 83.7 us; the launch traced here: 83.4 us
  Pallas kernels  76.4 us (91%)
  local copies, waits for them, and re-layouts  6.17 us (7%)
    pallas_call x1, Pallas kernels, per_device(): pl.pallas_call(functools.partial(return_kernel, num_blk, num_col), out_sh...  29.8 us
    pallas_call x1, Pallas kernels, per_device(): pl.pallas_call(functools.partial(halo_kernel, num_blk, num_col), out_shap...  20.8 us
    pallas_call x2, Pallas kernels, swap(): pl.pallas_call(functools.partial(swap_kernel, num_blk, num_col), out_shap...  14.9 us
    unnamed x18, local copies, waits for them, and re-layouts  4.64 us
    pallas_call x1, Pallas kernels, per_device(): pl.pallas_call(functools.partial(aggregate_kernel, slots), grid=(steps,),...  3.27 us
    pallas_call x1, Pallas kernels, per_device(): pl.pallas_call(functools.partial(spread_kernel, slots), grid=(steps,), ou...  2.48 us
    pallas_call x1, Pallas kernels, per_device(): pl.pallas_call(functools.partial(dense_kernel, min(part, 256)), out_shape...  2.36 us
    pallas_call x1, Pallas kernels, per_device(): pl.pallas_call(finish_kernel, out_shape=shape((dim, rows), half), in_spec...  1.89 us

profile of v1, /device:TPU:0, one launch (start us, length us, event | category | flops | bytes accessed | tf_op | source)
XLA Modules:
  0.0 83.4 jit_solution(15179899206288480435)
XLA Ops:
  0.6 0.0 copy-start.7
  0.6 0.0 copy-start.6
  0.7 0.8 copy.17.send_ref
  1.4 0.8 copy.16.bias_ref
  2.2 0.0 copy-start.1
  2.2 1.0 %copy-done.1 = bf16[128,2048]{1,0:T(8,128)(2,1)S(1)} copy-done((bf16[128,2048]{1,0:T(8,128)(2,1)S(1)}, bf16[128,2048]{1,0:T(8,128)(2,1)}, u32[]{:S(2)}) %copy-start.1) | copy-done | bytes 524312
  3.3 0.0 copy-start
  3.3 0.9 %pack.1.sbuf = bf16[8,128,512]{2,1,0:T(8,128)(2,1)S(1)} custom-call(s32[1,8,4]{2,1,0:T(8,128)S(1)} %copy.17.send_ref, bf16[128,2048]{1,0:T(8,128)(2,1)S(1)} %copy-done.1), custom_call_target="tpu_custom_call" | custom-call | tf_op jit(solution)/shard_map/pack/pallas_call | solution.py:346
  4.2 0.0 copy-start.2
  4.2 1.2 %copy-done.2 = bf16[128,2048]{1,0:T(8,128)(2,1)S(1)} copy-done((bf16[128,2048]{1,0:T(8,128)(2,1)S(1)}, bf16[128,2048]{1,0:T(8,128)(2,1)}, u32[]{:S(2)}) %copy-start.2) | copy-done | bytes 524312
  5.4 0.0 copy-start.3
  5.4 1.0 %copy-done.3 = bf16[128,2048]{1,0:T(8,128)(2,1)S(1)} copy-done((bf16[128,2048]{1,0:T(8,128)(2,1)S(1)}, bf16[128,2048]{1,0:T(8,128)(2,1)}, u32[]{:S(2)}) %copy-start.3) | copy-done | bytes 524312
  6.5 20.8 %halo.1 = (bf16[8,128,512]{2,1,0:T(8,128)(2,1)S(1)}, bf16[2,128,1024]{2,1,0:T(8,128)(2,1)S(1)}, bf16[2,128,1024]{2,1,0:T(8,128)(2,1)S(1)}) custom-call(bf16[8,128,512]{2,1,0:T(8,128)(2,1)S(1)} %pack.1.sbuf, bf16[128,2048]{1,0:T(8,128)(2,1)S(1)} %copy-done.2, bf16[128,2048]{1,0:T(8,128)(2,1)S(1)} %copy-done.3), custom_call_target="tpu_custom_call" | custom-call | tf_op jit(solution)/shard_map/halo/pallas_call | solution.py:354
  27.3 0.0 copy-start.4
  27.3 0.0 copy-start.5
  27.3 0.0 copy-done.7
  27.4 0.0 copy-done.6
  27.4 0.0 copy-done
  27.4 3.3 %aggregate.1 = (bf16[2,128,1024]{2,1,0:T(8,128)(2,1)S(1)}, f32[2,1,1024]{2,1,0:T(1,128)S(1)}) custom-call(s32[56]{0:T(128)S(1)} %copy-done.6, s32[56]{0:T(128)S(1)} %copy-done.7, bf16[128,2048]{1,0:T(8,128)(2,1)S(1)} %copy-done.2, bf16[8,128,512]{2,1,0:T(8,128)(2,1)S(1)} %get-tuple-element.19.recv_ref, s32[56,128,128]{2,1,0:T(8,128)S(1)} %copy-done), custom_call_target="tpu_custom_call" | custom-call | tf_op jit(solution)/shard_map/aggregate/pallas_call | solution.py:369
  30.7 7.9 %swap_aggregate.1 = bf16[2,128,1024]{2,1,0:T(8,128)(2,1)S(1)} custom-call(bf16[2,128,1024]{2,1,0:T(8,128)(2,1)S(1)} %get-tuple-element.20.src_ref), custom_call_target="tpu_custom_call" | custom-call | tf_op jit(solution)/shard_map/swap_aggregate/pallas_call | solution.py:381
  38.6 0.0 copy-done.4
  38.6 0.0 copy-done.5
  38.6 2.4 %dense.1 = (bf16[2,128,1024]{2,1,0:T(8,128)(2,1)S(1)}, bf16[2,128,1024]{2,1,0:T(8,128)(2,1)S(1)}, bf16[2,256,384]{2,1,0:T(8,128)(2,1)S(1)}) custom-call(bf16[256,1024]{1,0:T(8,128)(2,1)S(1)} %bitcast.9, bf16[256,1024]{1,0:T(8,128)(2,1)S(1)} %bitcast.8, bf16[256,1024]{1,0:T(8,128)(2,1)S(1)} %bitcast.10, f32[2,1,1024]{2,1,0:T(1,128)S(1)} %get-tuple-element.22.floor_ref, ...), custom_call_target="tpu_custom_call" | custom-call | tf_op jit(solution)/shard_map/dense/pallas_call | solution.py:393
  40.9 7.0 %swap_scaled.1.scaled_ref = bf16[2,128,1024]{2,1,0:T(8,128)(2,1)S(1)} custom-call(bf16[2,128,1024]{2,1,0:T(8,128)(2,1)S(1)} %get-tuple-element.23.src_ref), custom_call_target="tpu_custom_call" | custom-call | tf_op jit(solution)/shard_map/swap_scaled/pallas_call | solution.py:381
  48.0 2.5 %spread.1 = (bf16[8,128,512]{2,1,0:T(8,128)(2,1)S(1)}, f32[16,128,128]{2,1,0:T(8,128)S(1)}) custom-call(s32[56]{0:T(128)S(1)} %copy-done.6, s32[56]{0:T(128)S(1)} %copy-done.7, bf16[2,128,1024]{2,1,0:T(8,128)(2,1)S(1)} %swap_scaled.1.scaled_ref, s32[56,128,128]{2,1,0:T(8,128)S(1)} %copy-done), custom_call_target="tpu_custom_call" | custom-call | tf_op jit(solution)/shard_map/spread/pallas_call | solution.py:406
  50.4 29.8 %give_back.1 = (bf16[8,128,512]{2,1,0:T(8,128)(2,1)S(1)}, bf16[2,128,1024]{2,1,0:T(8,128)(2,1)S(1)}, bf16[16,16,256]{2,1,0:T(8,128)(2,1)S(1)}, f32[1,128]{1,0:T(1,128)S(1)}) custom-call(bf16[8,128,512]{2,1,0:T(8,128)(2,1)S(1)} %get-tuple-element.24.ret_ref, bf16[2,128,1024]{2,1,0:T(8,128)(2,1)S(1)} %get-tuple-element.25.self_ref, ...), custom_call_target="tpu_custom_call" | custom-call | tf_op jit(solution)/shard_map/give_back/pallas_call | solution.py:418
  80.3 1.9 %finish.1 = bf16[128,2048]{1,0:T(8,128)(2,1)} custom-call(s32[1,8,4]{2,1,0:T(8,128)S(1)} %copy.17.send_ref, bf16[2,128,1024]{2,1,0:T(8,128)(2,1)S(1)} %get-tuple-element.27.self_ref, f32[16,128,128]{2,1,0:T(8,128)S(1)} %get-tuple-element.28.back_ref, bf16[8,128,512]{2,1,0:T(8,128)(2,1)S(1)} %get-tuple-element.29.came_ref), custom_call_target="tpu_custom_call" | custom-call | tf_op jit(solution)/shard_map/finish/pallas_call | solution.py:435
  82.2 0.7 fusion
  82.9 0.5 copy.19
Async XLA Ops:
  0.6 26.7 %copy-start.7 = (s32[56]{0:T(128)S(1)}, s32[56]{0:T(128)}, u32[]{:S(2)}) copy-start(s32[56]{0:T(128)} %src_ref.3) | copy-start | bytes 676
  0.6 26.7 %copy-start.6 = (s32[56]{0:T(128)S(1)}, s32[56]{0:T(128)}, u32[]{:S(2)}) copy-start(s32[56]{0:T(128)} %dst_ref.3) | copy-start | bytes 676
  2.2 1.0 %copy-start.1 = (bf16[128,2048]{1,0:T(8,128)(2,1)S(1)}, bf16[128,2048]{1,0:T(8,128)(2,1)}, u32[]{:S(2)}) copy-start(bf16[128,2048]{1,0:T(8,128)(2,1)} %feat_ref.5) | copy-start | bytes 1572868
  3.3 24.1 %copy-start = (s32[56,128,128]{2,1,0:T(8,128)S(1)}, s32[56,128,128]{2,1,0:T(8,128)}, u32[]{:S(2)}) copy-start(s32[56,128,128]{2,1,0:T(8,128)} %cnt_ref.3) | copy-start | bytes 11010052
  4.2 1.3 %copy-start.2 = (bf16[128,2048]{1,0:T(8,128)(2,1)S(1)}, bf16[128,2048]{1,0:T(8,128)(2,1)}, u32[]{:S(2)}) copy-start(bf16[128,2048]{1,0:T(8,128)(2,1)} %feat_ref.5) | copy-start | bytes 1572868
  5.4 1.0 %copy-start.3 = (bf16[128,2048]{1,0:T(8,128)(2,1)S(1)}, bf16[128,2048]{1,0:T(8,128)(2,1)}, u32[]{:S(2)}) copy-start(bf16[128,2048]{1,0:T(8,128)(2,1)} %cot_ref.1) | copy-start | bytes 1572868
  27.3 11.2 %copy-start.4 = (bf16[256,256]{1,0:T(8,128)(2,1)S(1)}, bf16[256,256]{1,0:T(8,128)(2,1)}, u32[]{:S(2)}) copy-start(bf16[256,256]{1,0:T(8,128)(2,1)} %ws_ref.1) | copy-start | bytes 393220
  27.3 11.2 %copy-start.5 = (bf16[256,256]{1,0:T(8,128)(2,1)S(1)}, bf16[256,256]{1,0:T(8,128)(2,1)}, u32[]{:S(2)}) copy-start(bf16[256,256]{1,0:T(8,128)(2,1)} %wn_ref.1) | copy-start | bytes 393220

commit v2 on v1

--- a/solution.py
+++ b/solution.py
@@ -117,7 +117,8 @@
         copy.wait()
 
 
-def aggregate_kernel(slots, dst_ref, src_ref, feat_ref, recv_ref, cnt_ref, agg_ref, floor_ref, acc):
+def aggregate_kernel(slots, dst_ref, src_ref, feat_ref, recv_ref, cnt_ref, agg_ref, floor_ref,
+                     half_ref, slot_dst_ref, acc):
     step = pl.program_id(0)
     blocks, rows, side = acc.shape
     dim = feat_ref.shape[0]
@@ -129,8 +130,9 @@
     def _():
         acc[...] = jnp.zeros_like(acc)
 
-    def add(tile, picked):
+    def add(tile, picked, place):
         counts = cnt_ref[tile].astype(jnp.float32).astype(jnp.bfloat16)
+        half_ref[place] = counts
         left = jnp.concatenate([picked, jnp.ones((rows - dim, side), jnp.bfloat16)], axis=0)
         product = lax.dot_general(
             left, counts, (((1,), (1,)), ((), ())), preferred_element_type=jnp.float32
@@ -143,13 +145,14 @@
         for tile in range(tiles):
             slot = src_ref[step * tiles + tile] - blocks
             start = pl.multiple_of(lax.rem(slot, cap) * side, side)
-            add(tile, recv_ref[lax.div(slot, cap), :, pl.ds(start, side)])
+            add(tile, recv_ref[lax.div(slot, cap), :, pl.ds(start, side)], slot)
+            slot_dst_ref[slot] = dst_ref[step * tiles + tile]
 
     @pl.when(step * tiles >= slots)
     def _():
         for tile in range(tiles):
             start = pl.multiple_of(src_ref[step * tiles + tile] * side, side)
-            add(tile, feat_ref[:, pl.ds(start, side)])
+            add(tile, feat_ref[:, pl.ds(start, side)], step * tiles + tile)
 
     @pl.when(step == pl.num_programs(0) - 1)
     def _():
@@ -177,10 +180,12 @@
 
 def dense_kernel(
     chunk, feat_ref, agg_ref, cot_ref, floor_ref, ws_ref, wn_ref, bias_ref,
-    scaled_ref, self_ref, grad_ref, acc,
+    *outs,
 ):
+    scaled_refs, (self_ref, grad_ref, acc) = outs[:-3], outs[-3:]
     width, nodes = feat_ref.shape
-    parts, dim, _ = scaled_ref.shape
+    parts, _, piece, side = scaled_refs[0].shape
+    dim = self_ref.shape[1]
     col = lax.axis_index("col")
     self_weight, neigh_weight = ws_ref[...], wn_ref[...]
     first = (((0,), (0,)), ((), ()))
@@ -200,7 +205,12 @@
         own = jnp.dot(self_weight, dz, preferred_element_type=jnp.float32)
         for part in range(parts):
             rows = slice(part * dim, (part + 1) * dim)
-            scaled_ref[part, :, at] = neigh[rows].astype(jnp.bfloat16)
+            for index, scaled_ref in enumerate(scaled_refs):
+                top = part * dim + index * piece
+                for left in range(0, chunk, side):
+                    scaled_ref[part, (start + left) // side] = neigh[
+                        top : top + piece, left : left + side
+                    ].astype(jnp.bfloat16)
             self_ref[part, :, at] = own[rows].astype(jnp.bfloat16)
         ones = jnp.ones((16, chunk), jnp.bfloat16)
         left = jnp.concatenate([feat, agg, ones], axis=0)
@@ -222,102 +232,126 @@
             grad_ref[part, :, width + dim :] = jnp.zeros((2 * dim, rest), jnp.bfloat16)
 
 
-def spread_kernel(slots, dst_ref, src_ref, scaled_ref, cnt_ref, ret_ref, back_ref):
-    step = pl.program_id(0)
-    num_hops, _, width = ret_ref.shape
+def return_kernel(
+    num_blk, num_col, slot_dst, half_ref, scaled_a, scaled_b, self_ref, grad_ref,
+    all_a, all_b, came_ref, self_all, grad_out, bias_out,
+    ret, col_buf, core_src, core_buf, mid_src, mid_buf, far_src, far_buf,
+    halo_send, halo_recv, col_send, col_recv, up_send, up_recv, down_send, down_recv, own_sem,
+):
+    slots = ret.shape[1]
+    num_hops = halo_send.shape[1]
     cap = slots // num_hops
-    side = width // cap
-    blocks = back_ref.shape[0]
-    per_part = scaled_ref.shape[2] // side
-    tiles = cnt_ref.shape[0]
-
-    @pl.when(step == 0)
-    def _():
-        back_ref[...] = jnp.zeros_like(back_ref)
-
-    def contribution(tile):
-        dst = dst_ref[step * tiles + tile]
-        start = pl.multiple_of(lax.rem(dst, per_part) * side, side)
-        picked = scaled_ref[lax.div(dst, per_part), :, pl.ds(start, side)]
-        counts = cnt_ref[tile].astype(jnp.float32).astype(jnp.bfloat16)
-        return jnp.dot(picked, counts, preferred_element_type=jnp.float32)
-
-    @pl.when(step * tiles < slots)
-    def _():
-        for tile in range(tiles):
-            slot = src_ref[step * tiles + tile] - blocks
-            start = pl.multiple_of(lax.rem(slot, cap) * side, side)
-            ret_ref[lax.div(slot, cap), :, pl.ds(start, side)] = contribution(tile).astype(
-                jnp.bfloat16
+    blocks = scaled_a.shape[1]
+    row, col, col_peer = positions(num_blk, num_col)
+    far_size = num_blk // 4
+    core, mid, far = row % 2, (row // 2) % 2, row // 4
+    width = grad_out.shape[4]
+    halo = halo_peers(row, col, num_blk, num_hops, -1)
+    core_peer = (far * 4 + mid * 2 + 1 - core, col)
+    mid_peer = (far * 4 + (1 - mid) * 2 + core, col)
+    far_peers = [((far + step) % far_size * 4 + mid * 2 + core, col) for step in range(1, far_size)]
+    greet(halo + [core_peer, mid_peer] + far_peers + col_peer)
+
+    def across(at, source, target):
+        return [
+            push(source.at[peer[1]], target(step), col_send.at[at, step], col_recv.at[at, step], peer)
+            for step, peer in enumerate(col_peer)
+        ]
+
+    def settle(copies):
+        for copy in copies:
+            copy.wait()
+
+    mine = pl.ds(col * blocks, blocks)
+    owns = []
+    for at, (source, target) in enumerate(
+        ((scaled_a.at[col], all_a.at[mine]), (scaled_b.at[col], all_b.at[mine]), (self_ref.at[col], self_all.at[col]))
+    ):
+        own = pltpu.make_async_copy(source, target, own_sem.at[at])
+        own.start()
+        owns.append(own)
+    grads = across(0, grad_ref, lambda step: col_buf.at[step])
+    ins = [across(1, scaled_a, lambda step: all_a.at[mine]), across(2, scaled_b, lambda step: all_b.at[mine])]
+
+    def spread(index, source):
+        def body(slot, carry):
+            picked = source[slot_dst[slot]]
+            ret[index, slot] = jnp.dot(
+                picked, half_ref[slot], preferred_element_type=jnp.float32
+            ).astype(jnp.bfloat16)
+            return carry
+
+        lax.fori_loop(0, slots, body, 0, unroll=8)
+
+    def give(index):
+        copies = []
+        for at in range(num_hops):
+            part = pl.ds(at * cap, cap)
+            copies.append(
+                push(
+                    ret.at[index, part], came_ref.at[index, part], halo_send.at[index, at],
+                    halo_recv.at[index, at], halo[at],
+                )
             )
-
-    @pl.when(step * tiles >= slots)
-    def _():
-        for tile in range(tiles):
-            back_ref[src_ref[step * tiles + tile]] += contribution(tile)
-
-
-def return_kernel(
-    num_blk, num_col, ret_ref, self_ref, grad_ref, came_ref, self_all, grad_out, bias_out,
-    col_buf, rs_src, rs_buf, piece,
-    halo_send, halo_recv, col_send, col_recv, rs_send, rs_recv, ag_send, ag_recv, own_sem,
+        return copies
+
+    settle(grads)
+    total = grad_ref[col].astype(jnp.float32)
+    for step in range(num_col - 1):
+        total += col_buf[step].astype(jnp.float32)
+    core_src[...] = total.astype(jnp.bfloat16)
+    up = push(core_src.at[1 - core], core_buf, up_send.at[0], up_recv.at[0], core_peer)
+    settle(ins[0])
+    owns[0].wait()
+    spread(0, all_a)
+    up.wait()
+    mid_src[...] = (core_src[core].astype(jnp.float32) + core_buf[...].astype(jnp.float32)).astype(jnp.bfloat16)
+    up = push(mid_src.at[1 - mid], mid_buf, up_send.at[1], up_recv.at[1], mid_peer)
+    later = give(0)
+    later += across(3, self_ref, lambda step: self_all.at[col])
+    up.wait()
+    far_src[...] = (mid_src[mid].astype(jnp.float32) + mid_buf[...].astype(jnp.float32)).astype(jnp.bfloat16)
+    ups = [
+        push(far_src.at[peer[0] // 4], far_buf.at[step], up_send.at[2 + step], up_recv.at[2 + step], peer)
+        for step, peer in enumerate(far_peers)
+    ]
+    settle(ins[1])
+    owns[1].wait()
+    spread(1, all_b)
+    later += give(1)
+    settle(ups)
+    total = far_src[far].astype(jnp.float32)
+    for step in range(far_size - 1):
+        total += far_buf[step].astype(jnp.float32)
+    bias_out[...] = total[0:1, width:]
+    grad_out[core, mid, far] = total[:, :width].astype(jnp.bfloat16)
+    settle([
+        push(
+            grad_out.at[core, mid, far], grad_out.at[core, mid, far], down_send.at[2 + step],
+            down_recv.at[2 + step], peer,
+        )
+        for step, peer in enumerate(far_peers)
+    ])
+    settle([push(grad_out.at[core, mid], grad_out.at[core, mid], down_send.at[1], down_recv.at[1], mid_peer)])
+    settle([push(grad_out.at[core], grad_out.at[core], down_send.at[0], down_recv.at[0], core_peer)])
+    settle(later)
+    owns[2].wait()
+
+
+def finish_kernel(
+    slots, send_ref, dst_ref, src_ref, half_ref, all_a, all_b, self_ref, came_ref, out_ref, acc
 ):
-    num_hops = ret_ref.shape[0]
-    row, col, col_peer = positions(num_blk, num_col)
-    width = piece.shape[1]
-    halo = halo_peers(row, col, num_blk, num_hops, -1)
-    ring = [(lax.rem(row + step, num_blk), col) for step in range(1, num_blk)]
-    greet(ring + col_peer)
-    first = [
-        push(grad_ref.at[peer[1]], col_buf.at[step], col_send.at[0, step], col_recv.at[0, step], peer)
-        for step, peer in enumerate(col_peer)
-    ]
-    later = [
-        push(ret_ref.at[index], came_ref.at[index], halo_send.at[index], halo_recv.at[index], halo[index])
-        for index in range(num_hops)
-    ]
-    later += [
-        push(self_ref.at[peer[1]], self_all.at[col], col_send.at[1, step], col_recv.at[1, step], peer)
-        for step, peer in enumerate(col_peer)
-    ]
-    own = pltpu.make_async_copy(self_ref.at[col], self_all.at[col], own_sem)
-    own.start()
-    for copy in first:
-        copy.wait()
-    for index in range(num_blk):
-        total = grad_ref[col, index].astype(jnp.float32)
-        for step in range(num_col - 1):
-            total += col_buf[step, index].astype(jnp.float32)
-        rs_src[index] = total.astype(jnp.bfloat16)
-    scatter = [
-        push(rs_src.at[peer[0]], rs_buf.at[step], rs_send.at[step], rs_recv.at[step], peer)
-        for step, peer in enumerate(ring)
-    ]
-    total = rs_src[row].astype(jnp.float32)
-    for step, copy in enumerate(scatter):
-        copy.wait()
-        total += rs_buf[step].astype(jnp.float32)
-    bias_out[...] = total[0:1, width:]
-    piece[...] = total[:, :width].astype(jnp.bfloat16)
-    grad_out[row] = piece[...]
-    gather = [
-        push(piece, grad_out.at[row], ag_send.at[step], ag_recv.at[step], peer)
-        for step, peer in enumerate(ring)
-    ]
-    for copy in gather + later:
-        copy.wait()
-    own.wait()
-
-
-def finish_kernel(send_ref, self_ref, back_ref, came_ref, out_ref, acc):
     blocks, _, side = acc.shape
-    num_hops, _, width = came_ref.shape
-    cap = width // side
-    acc[...] = back_ref[...]
-    for index in range(num_hops):
-        for slot in range(cap):
-            came = came_ref[index, :, slot * side : (slot + 1) * side]
-            acc[send_ref[0, index, slot]] += came.astype(jnp.float32)
+    num_hops, cap = send_ref.shape[1:]
+    piece = all_a.shape[1]
+    acc[...] = jnp.zeros_like(acc)
+    for tile in range(slots, dst_ref.shape[0]):
+        dst = dst_ref[tile]
+        picked = jnp.concatenate([all_a[dst], all_b[dst]], axis=0)
+        acc[src_ref[tile]] += jnp.dot(picked, half_ref[tile], preferred_element_type=jnp.float32)
+    for slot in range(slots):
+        came = jnp.concatenate([came_ref[0, slot], came_ref[1, slot]], axis=0)
+        acc[send_ref[0, slot // cap, slot % cap]] += came.astype(jnp.float32)
     per_part = self_ref.shape[2] // side
     for block in range(blocks):
         at = (block % per_part) * side
@@ -366,12 +400,15 @@
     steps = tiles // STEP_TILES
     cnt_spec = pl.BlockSpec((STEP_TILES, side, side), lambda step: (step, 0, 0))
     whole = lambda dims: pl.BlockSpec(dims, lambda step: (0,) * len(dims))
-    aggregate, floor = pl.pallas_call(
+    aggregate, floor, half_cnt, slot_dst = pl.pallas_call(
         functools.partial(aggregate_kernel, slots),
         grid=(steps,),
-        out_shape=(split, shape((num_col, 1, part), full)),
+        out_shape=(
+            split, shape((num_col, 1, part), full), shape((tiles, side, side), half),
+            shape((slots,), jnp.int32),
+        ),
         in_specs=[smem(), smem(), whole((dim, rows)), whole(slot_shape.shape), cnt_spec],
-        out_specs=(whole(split.shape), whole((num_col, 1, part))),
+        out_specs=(whole(split.shape), whole((num_col, 1, part)), whole((tiles, side, side)), smem()),
         scratch_shapes=[pltpu.VMEM((blocks, dim + 16, side), full)],
         compiler_params=params(),
         name="aggregate",
@@ -390,11 +427,14 @@
 
     agg_all = swap(aggregate, 1, "swap_aggregate")
     lanes = width + 128
-    scaled, own_part, grads = pl.pallas_call(
+    per_part = part // side
+    piece = dim // 2
+    scaled_shape = shape((num_col, per_part, piece, side), half)
+    scaled_a, scaled_b, own_part, grads = pl.pallas_call(
         functools.partial(dense_kernel, min(part, 256)),
-        out_shape=(split, split, shape((num_col, 2 * dim, lanes), half)),
+        out_shape=(scaled_shape, scaled_shape, split, shape((num_col, 2 * dim, lanes), half)),
         in_specs=[vmem()] * 7,
-        out_specs=(vmem(),) * 3,
+        out_specs=(vmem(),) * 4,
         scratch_shapes=[pltpu.VMEM((2 * width + 16, width), full)],
         compiler_params=params(),
         name="dense",
@@ -402,45 +442,43 @@
         feat_all.reshape(width, part), agg_all.reshape(width, part), cot_all.reshape(width, part),
         floor, self_weight, neigh_weight, bias.reshape(width, 1),
     )
-    scaled_all = swap(scaled, 2, "swap_scaled")
-    returning, back_local = pl.pallas_call(
-        functools.partial(spread_kernel, slots),
-        grid=(steps,),
-        out_shape=(slot_shape, shape((blocks, dim, side), full)),
-        in_specs=[smem(), smem(), whole(split.shape), cnt_spec],
-        out_specs=(whole(slot_shape.shape), whole((blocks, dim, side))),
-        compiler_params=params(),
-        name="spread",
-    )(tile_dst, tile_src, scaled_all, tile_cnt)
-
+
+    far_size = num_blk // 4
     span = 2 * dim // num_blk
-    ring = num_blk - 1
-    came, own_all, grad_sum, bias_sum = pl.pallas_call(
+    all_shape = shape((blocks, piece, side), half)
+    level = lambda *lead: pltpu.VMEM(lead + (span, lanes), half)
+    all_a, all_b, came, own_all, grad_sum, bias_sum = pl.pallas_call(
         functools.partial(return_kernel, num_blk, num_col),
-        out_shape=(slot_shape, split, shape((num_blk, span, width), half), shape((1, 128), full)),
-        in_specs=[anywhere(), anywhere(), vmem()],
-        out_specs=(anywhere(), anywhere(), vmem(), vmem()),
+        out_shape=(
+            all_shape, all_shape, shape((2, slots, piece, side), half), split,
+            shape((2, 2, far_size, span, width), half), shape((1, 128), full),
+        ),
+        in_specs=[smem()] + [vmem()] * 5,
+        out_specs=(vmem(),) * 6,
         scratch_shapes=[
-            pltpu.VMEM((peers, num_blk, span, lanes), half),
-            pltpu.VMEM((num_blk, span, lanes), half),
-            pltpu.VMEM((ring, span, lanes), half),
-            pltpu.VMEM((span, width), half),
-            dma((num_hops,)), dma((num_hops,)), dma((2, peers)), dma((2, peers)),
-            dma((ring,)), dma((ring,)), dma((ring,)), dma((ring,)), dma(()),
+            pltpu.VMEM((2, slots, piece, side), half),
+            level(peers, 2, 2, far_size), level(2, 2, far_size), level(2, far_size),
+            level(2, far_size), level(far_size), level(far_size), level(max(far_size - 1, 1)),
+            dma((2, num_hops)), dma((2, num_hops)), dma((4, peers)), dma((4, peers)),
+            dma((far_size + 1,)), dma((far_size + 1,)), dma((far_size + 1,)), dma((far_size + 1,)),
+            dma((3,)),
         ],
-        compiler_params=params(3),
+        compiler_params=params(2),
         name="give_back",
-    )(returning, own_part, grads.reshape(num_col, num_blk, span, lanes))
+    )(
+        slot_dst, half_cnt, scaled_a, scaled_b, own_part,
+        grads.reshape(num_col, 2, 2, far_size, span, lanes),
+    )
 
     grad_feats = pl.pallas_call(
-        finish_kernel,
+        functools.partial(finish_kernel, slots),
         out_shape=shape((dim, rows), half),
-        in_specs=[smem(), vmem(), vmem(), vmem()],
+        in_specs=[smem()] * 3 + [vmem()] * 5,
         out_specs=vmem(),
         scratch_shapes=[pltpu.VMEM((blocks, dim, side), full)],
         compiler_params=params(),
         name="finish",
-    )(send_blk, own_all, back_local, came)
+    )(send_blk, tile_dst, tile_src, half_cnt, all_a, all_b, own_all, came)
     grad_both = grad_sum.reshape(2 * dim, width).astype(full)
     return (grad_feats, grad_both[:dim], grad_both[dim:], bias_sum[0, :dim])
 

time: 83.7 us -> 84.4 us (level)
  local copies, waits for them, and re-layouts: 6.17 us -> 7.98 us
  Pallas kernels: 76.4 us -> 75.3 us
    pallas_call x1, Pallas kernels: 29.8 us -> 37.2 us  [per_device(): pl.pallas_call(functools.partial(return_kernel, num_blk, num_col), out_sh...]
    pallas_call x2 -> x1, Pallas kernels: 14.9 us -> 7.91 us  [swap(): pl.pallas_call(functools.partial(swap_kernel, num_blk, num_col), out_shap...]
    pallas_call x2 -> x1, Pallas kernels: 4.37 us -> 2.19 us  [per_device(): pl.pallas_call(functools.partial(finish_kernel, slots), out_shape=shape((...]
    unnamed x18, local copies, waits for them, and re-layouts: 4.64 us -> 6.45 us
where the time goes in v2:
time: 84.4 us; the launch traced here: 84.1 us
  Pallas kernels  75.3 us (89%)
  local copies, waits for them, and re-layouts  7.98 us (9%)
    pallas_call x1, Pallas kernels, per_device(): pl.pallas_call(functools.partial(return_kernel, num_blk, num_col), out_sh...  37.2 us
    pallas_call x1, Pallas kernels, per_device(): pl.pallas_call(functools.partial(halo_kernel, num_blk, num_col), out_shap...  20.8 us
    pallas_call x1, Pallas kernels, swap(): pl.pallas_call(functools.partial(swap_kernel, num_blk, num_col), out_shap...  7.91 us
    unnamed x18, local copies, waits for them, and re-layouts  6.45 us
    pallas_call x1, Pallas kernels, per_device(): pl.pallas_call(functools.partial(aggregate_kernel, slots), grid=(steps,),...  3.98 us
    pallas_call x1, Pallas kernels, per_device(): pl.pallas_call(functools.partial(dense_kernel, min(part, 256)), out_shape...  2.34 us
    pallas_call x1, Pallas kernels, per_device(): pl.pallas_call(functools.partial(finish_kernel, slots), out_shape=shape((...  2.19 us

profile of v2, /device:TPU:0, one launch (start us, length us, event | category | flops | bytes accessed | tf_op | source)
XLA Modules:
  0.0 84.1 jit_solution(14139335897968624180)
XLA Ops:
  0.6 0.0 copy-start.7
  0.6 0.0 copy-start.6
  0.7 0.8 copy.17.send_ref
  1.4 0.8 copy.16.bias_ref
  2.2 0.0 copy-start
  2.2 1.0 %copy-done = bf16[128,2048]{1,0:T(8,128)(2,1)S(1)} copy-done((bf16[128,2048]{1,0:T(8,128)(2,1)S(1)}, bf16[128,2048]{1,0:T(8,128)(2,1)}, u32[]{:S(2)}) %copy-start) | copy-done | bytes 524312
  3.3 0.9 %pack.1.sbuf = bf16[8,128,512]{2,1,0:T(8,128)(2,1)S(1)} custom-call(s32[1,8,4]{2,1,0:T(8,128)S(1)} %copy.17.send_ref, bf16[128,2048]{1,0:T(8,128)(2,1)S(1)} %copy-done), custom_call_target="tpu_custom_call" | custom-call | tf_op jit(solution)/shard_map/pack/pallas_call | solution.py:380
  4.2 0.0 copy-start.1
  4.2 1.0 %copy-done.1 = bf16[128,2048]{1,0:T(8,128)(2,1)S(1)} copy-done((bf16[128,2048]{1,0:T(8,128)(2,1)S(1)}, bf16[128,2048]{1,0:T(8,128)(2,1)}, u32[]{:S(2)}) %copy-start.1) | copy-done | bytes 524312
  5.2 0.0 copy-start.3
  5.2 1.0 %copy-done.3 = bf16[128,2048]{1,0:T(8,128)(2,1)S(1)} copy-done((bf16[128,2048]{1,0:T(8,128)(2,1)S(1)}, bf16[128,2048]{1,0:T(8,128)(2,1)}, u32[]{:S(2)}) %copy-start.3) | copy-done | bytes 524312
  6.2 0.0 copy-start.4
  6.3 0.0 copy-start.5
  6.3 20.8 %halo.1 = (bf16[8,128,512]{2,1,0:T(8,128)(2,1)S(1)}, bf16[2,128,1024]{2,1,0:T(8,128)(2,1)S(1)}, bf16[2,128,1024]{2,1,0:T(8,128)(2,1)S(1)}) custom-call(bf16[8,128,512]{2,1,0:T(8,128)(2,1)S(1)} %pack.1.sbuf, bf16[128,2048]{1,0:T(8,128)(2,1)S(1)} %copy-done.1, bf16[128,2048]{1,0:T(8,128)(2,1)S(1)} %copy-done.3), custom_call_target="tpu_custom_call" | custom-call | tf_op jit(solution)/shard_map/halo/pallas_call | solution.py:388
  27.1 0.0 copy-done.7
  27.1 0.0 copy-done.6
  27.1 0.0 copy-start.2
  27.1 2.0 %copy-done.2 = s32[56,128,128]{2,1,0:T(8,128)S(1)} copy-done((s32[56,128,128]{2,1,0:T(8,128)S(1)}, s32[56,128,128]{2,1,0:T(8,128)}, u32[]{:S(2)}) %copy-start.2) | copy-done | bytes 3670040
  29.2 4.0 %aggregate.1 = (bf16[2,128,1024]{2,1,0:T(8,128)(2,1)S(1)}, f32[2,1,1024]{2,1,0:T(1,128)S(1)}, bf16[56,128,128]{2,1,0:T(8,128)(2,1)S(1)}, s32[32]{0:T(128)S(1)}) custom-call(s32[56]{0:T(128)S(1)} %copy-done.6, s32[56]{0:T(128)S(1)} %copy-done.7, bf16[128,2048]{1,0:T(8,128)(2,1)S(1)} %copy-done.1, bf16[8,128,512]{2,1,0:T(8,128)(2,1)S(1)} %get-tuple-element.21.recv_ref, ...), custom_call_target="tpu_custom_call" | custom-call | tf_op jit(solution)/shard_map/aggregate/pallas_call | solution.py:403
  33.2 7.9 %swap_aggregate.1 = bf16[2,128,1024]{2,1,0:T(8,128)(2,1)S(1)} custom-call(bf16[2,128,1024]{2,1,0:T(8,128)(2,1)S(1)} %get-tuple-element.25.src_ref), custom_call_target="tpu_custom_call" | custom-call | tf_op jit(solution)/shard_map/swap_aggregate/pallas_call | solution.py:418
  41.1 0.0 copy-done.4
  41.1 0.0 copy-done.5
  41.1 2.3 %dense.1 = (bf16[2,8,64,128]{3,2,1,0:T(8,128)(2,1)S(1)}, bf16[2,8,64,128]{3,2,1,0:T(8,128)(2,1)S(1)}, bf16[2,128,1024]{2,1,0:T(8,128)(2,1)S(1)}, bf16[2,256,384]{2,1,0:T(8,128)(2,1)S(1)}) custom-call(bf16[256,1024]{1,0:T(8,128)(2,1)S(1)} %bitcast.9, bf16[256,1024]{1,0:T(8,128)(2,1)S(1)} %bitcast.8, bf16[256,1024]{1,0:T(8,128)(2,1)S(1)} %bitcast.10, ...), custom_call_target="tpu_custom_call" | custom-call | tf_op jit(solution)/shard_map/dense/pallas_call | solution.py:433
  43.4 37.2 %give_back.1 = (bf16[16,64,128]{2,1,0:T(8,128)(2,1)S(1)}, bf16[16,64,128]{2,1,0:T(8,128)(2,1)S(1)}, bf16[2,32,64,128]{3,2,1,0:T(8,128)(2,1)S(1)}, bf16[2,128,102...) custom-call(s32[32]{0:T(128)S(1)} %get-tuple-element.23.slot_dst, ...), custom_call_target="tpu_custom_call" | custom-call | tf_op jit(solution)/shard_map/give_back/pallas_call | solution.py:450
  80.6 2.2 %finish.1 = bf16[128,2048]{1,0:T(8,128)(2,1)} custom-call(s32[1,8,4]{2,1,0:T(8,128)S(1)} %copy.17.send_ref, s32[56]{0:T(128)S(1)} %copy-done.6, s32[56]{0:T(128)S(1)} %copy-done.7, bf16[56,128,128]{2,1,0:T(8,128)(2,1)S(1)} %get-tuple-element.22.half_ref, bf16[16,64,128]{2,1,0:T(8,128)(2,1)S(1)} %get-tuple-element.32.all_a, ...), custom_call_target="tpu_custom_call" | custom-call | tf_op jit(solution)/shard_map/finish/pallas_call | solution.py:473
  82.8 0.7 fusion
  83.5 0.5 copy.19
Async XLA Ops:
  0.6 26.5 %copy-start.7 = (s32[56]{0:T(128)S(1)}, s32[56]{0:T(128)}, u32[]{:S(2)}) copy-start(s32[56]{0:T(128)} %src_ref.3) | copy-start | bytes 676
  0.6 26.5 %copy-start.6 = (s32[56]{0:T(128)S(1)}, s32[56]{0:T(128)}, u32[]{:S(2)}) copy-start(s32[56]{0:T(128)} %dst_ref.3) | copy-start | bytes 676
  2.2 1.0 %copy-start = (bf16[128,2048]{1,0:T(8,128)(2,1)S(1)}, bf16[128,2048]{1,0:T(8,128)(2,1)}, u32[]{:S(2)}) copy-start(bf16[128,2048]{1,0:T(8,128)(2,1)} %feat_ref.5) | copy-start | bytes 1572868
  4.2 1.0 %copy-start.1 = (bf16[128,2048]{1,0:T(8,128)(2,1)S(1)}, bf16[128,2048]{1,0:T(8,128)(2,1)}, u32[]{:S(2)}) copy-start(bf16[128,2048]{1,0:T(8,128)(2,1)} %feat_ref.5) | copy-start | bytes 1572868
  5.2 1.0 %copy-start.3 = (bf16[128,2048]{1,0:T(8,128)(2,1)S(1)}, bf16[128,2048]{1,0:T(8,128)(2,1)}, u32[]{:S(2)}) copy-start(bf16[128,2048]{1,0:T(8,128)(2,1)} %cot_ref.1) | copy-start | bytes 1572868
  6.2 34.8 %copy-start.4 = (bf16[256,256]{1,0:T(8,128)(2,1)S(1)}, bf16[256,256]{1,0:T(8,128)(2,1)}, u32[]{:S(2)}) copy-start(bf16[256,256]{1,0:T(8,128)(2,1)} %ws_ref.1) | copy-start | bytes 393220
  6.3 34.8 %copy-start.5 = (bf16[256,256]{1,0:T(8,128)(2,1)S(1)}, bf16[256,256]{1,0:T(8,128)(2,1)}, u32[]{:S(2)}) copy-start(bf16[256,256]{1,0:T(8,128)(2,1)} %wn_ref.1) | copy-start | bytes 393220
  27.1 2.0 %copy-start.2 = (s32[56,128,128]{2,1,0:T(8,128)S(1)}, s32[56,128,128]{2,1,0:T(8,128)}, u32[]{:S(2)}) copy-start(s32[56,128,128]{2,1,0:T(8,128)} %cnt_ref.1) | copy-start | bytes 11010052

commit v3 on v2

--- a/solution.py
+++ b/solution.py
@@ -42,6 +42,10 @@
     return pltpu.CompilerParams(
         vmem_limit_bytes=VMEM_BYTES, collective_id=collective, has_side_effects=True
     )
+
+
+def added(one, other):
+    return one.astype(jnp.float32) + other.astype(jnp.float32)
 
 
 def positions(num_blk, num_col):
@@ -235,8 +239,9 @@
 def return_kernel(
     num_blk, num_col, slot_dst, half_ref, scaled_a, scaled_b, self_ref, grad_ref,
     all_a, all_b, came_ref, self_all, grad_out, bias_out,
-    ret, col_buf, core_src, core_buf, mid_src, mid_buf, far_src, far_buf,
-    halo_send, halo_recv, col_send, col_recv, up_send, up_recv, down_send, down_recv, own_sem,
+    ret, core_buf, mid_src, mid_buf, far_src, far_buf, side_src, side_buf,
+    halo_send, halo_recv, col_send, col_recv, core_send, core_recv, mid_send, mid_recv,
+    far_send, far_recv, down_send, down_recv, own_sem,
 ):
     slots = ret.shape[1]
     num_hops = halo_send.shape[1]
@@ -250,7 +255,8 @@
     core_peer = (far * 4 + mid * 2 + 1 - core, col)
     mid_peer = (far * 4 + (1 - mid) * 2 + core, col)
     far_peers = [((far + step) % far_size * 4 + mid * 2 + core, col) for step in range(1, far_size)]
-    greet(halo + [core_peer, mid_peer] + far_peers + col_peer)
+    cross_peer = (far * 4 + (1 - mid) * 2 + 1 - core, col)
+    greet(halo + [core_peer, mid_peer, cross_peer] + far_peers + col_peer)
 
     def across(at, source, target):
         return [
@@ -270,8 +276,11 @@
         own = pltpu.make_async_copy(source, target, own_sem.at[at])
         own.start()
         owns.append(own)
-    grads = across(0, grad_ref, lambda step: col_buf.at[step])
-    ins = [across(1, scaled_a, lambda step: all_a.at[mine]), across(2, scaled_b, lambda step: all_b.at[mine])]
+    first = across(1, scaled_a, lambda step: all_a.at[mine])
+    ups = [
+        push(grad_ref.at[part, 1 - core], core_buf.at[part], core_send.at[part], core_recv.at[part], core_peer)
+        for part in range(num_col)
+    ]
 
     def spread(index, source):
         def body(slot, carry):
@@ -295,27 +304,26 @@
             )
         return copies
 
-    settle(grads)
-    total = grad_ref[col].astype(jnp.float32)
-    for step in range(num_col - 1):
-        total += col_buf[step].astype(jnp.float32)
-    core_src[...] = total.astype(jnp.bfloat16)
-    up = push(core_src.at[1 - core], core_buf, up_send.at[0], up_recv.at[0], core_peer)
-    settle(ins[0])
+    settle(ups)
+    for part in range(num_col):
+        mid_src[part] = added(grad_ref[part, core], core_buf[part]).astype(jnp.bfloat16)
+    ups = [
+        push(mid_src.at[part, 1 - mid], mid_buf.at[part], mid_send.at[part], mid_recv.at[part], mid_peer)
+        for part in range(num_col)
+    ]
+    settle(first)
+    second = across(2, scaled_b, lambda step: all_b.at[mine])
     owns[0].wait()
     spread(0, all_a)
-    up.wait()
-    mid_src[...] = (core_src[core].astype(jnp.float32) + core_buf[...].astype(jnp.float32)).astype(jnp.bfloat16)
-    up = push(mid_src.at[1 - mid], mid_buf, up_send.at[1], up_recv.at[1], mid_peer)
-    later = give(0)
-    later += across(3, self_ref, lambda step: self_all.at[col])
-    up.wait()
-    far_src[...] = (mid_src[mid].astype(jnp.float32) + mid_buf[...].astype(jnp.float32)).astype(jnp.bfloat16)
+    settle(ups)
+    for part in range(num_col):
+        far_src[:, part] = added(mid_src[part, mid], mid_buf[part]).astype(jnp.bfloat16)
     ups = [
-        push(far_src.at[peer[0] // 4], far_buf.at[step], up_send.at[2 + step], up_recv.at[2 + step], peer)
+        push(far_src.at[peer[0] // 4], far_buf.at[step], far_send.at[step], far_recv.at[step], peer)
         for step, peer in enumerate(far_peers)
     ]
-    settle(ins[1])
+    later = give(0)
+    settle(second)
     owns[1].wait()
     spread(1, all_b)
     later += give(1)
@@ -323,17 +331,26 @@
     total = far_src[far].astype(jnp.float32)
     for step in range(far_size - 1):
         total += far_buf[step].astype(jnp.float32)
+    side_src[...] = total.astype(jnp.bfloat16)
+    ups = across(0, side_src, lambda step: side_buf.at[step])
+    later += across(3, self_ref, lambda step: self_all.at[col])
+    settle(ups)
+    total = side_src[col].astype(jnp.float32)
+    for step in range(num_col - 1):
+        total += side_buf[step].astype(jnp.float32)
     bias_out[...] = total[0:1, width:]
     grad_out[core, mid, far] = total[:, :width].astype(jnp.bfloat16)
     settle([
         push(
-            grad_out.at[core, mid, far], grad_out.at[core, mid, far], down_send.at[2 + step],
-            down_recv.at[2 + step], peer,
+            grad_out.at[core, mid, far], grad_out.at[core, mid, far], down_send.at[3 + step],
+            down_recv.at[3 + step], peer,
         )
         for step, peer in enumerate(far_peers)
     ])
-    settle([push(grad_out.at[core, mid], grad_out.at[core, mid], down_send.at[1], down_recv.at[1], mid_peer)])
-    settle([push(grad_out.at[core], grad_out.at[core], down_send.at[0], down_recv.at[0], core_peer)])
+    settle([
+        push(grad_out.at[core, mid], grad_out.at[core, mid], down_send.at[at], down_recv.at[at], peer)
+        for at, peer in enumerate((core_peer, mid_peer, cross_peer))
+    ])
     settle(later)
     owns[2].wait()
 
@@ -457,10 +474,11 @@
         out_specs=(vmem(),) * 6,
         scratch_shapes=[
             pltpu.VMEM((2, slots, piece, side), half),
-            level(peers, 2, 2, far_size), level(2, 2, far_size), level(2, far_size),
-            level(2, far_size), level(far_size), level(far_size), level(max(far_size - 1, 1)),
+            level(num_col, 2, far_size), level(num_col, 2, far_size), level(num_col, far_size),
+            level(far_size, num_col), level(max(far_size - 1, 1), num_col), level(num_col), level(peers),
             dma((2, num_hops)), dma((2, num_hops)), dma((4, peers)), dma((4, peers)),
-            dma((far_size + 1,)), dma((far_size + 1,)), dma((far_size + 1,)), dma((far_size + 1,)),
+            dma((num_col,)), dma((num_col,)), dma((num_col,)), dma((num_col,)),
+            dma((far_size,)), dma((far_size,)), dma((far_size + 2,)), dma((far_size + 2,)),
             dma((3,)),
         ],
         compiler_params=params(2),

time: 84.4 us -> 80.4 us (0.953)
  Pallas kernels: 75.3 us -> 71.3 us
    pallas_call x1, Pallas kernels: 37.2 us -> 33.2 us  [per_device(): pl.pallas_call(functools.partial(return_kernel, num_blk, num_col), out_sh...]
where the time goes in v3:
time: 80.4 us; the launch traced here: 80 us
  Pallas kernels  71.3 us (89%)
  local copies, waits for them, and re-layouts  7.98 us (10%)
    pallas_call x1, Pallas kernels, per_device(): pl.pallas_call(functools.partial(return_kernel, num_blk, num_col), out_sh...  33.2 us
    pallas_call x1, Pallas kernels, per_device(): pl.pallas_call(functools.partial(halo_kernel, num_blk, num_col), out_shap...  20.8 us
    pallas_call x1, Pallas kernels, swap(): pl.pallas_call(functools.partial(swap_kernel, num_blk, num_col), out_shap...  7.91 us
    unnamed x18, local copies, waits for them, and re-layouts  6.45 us
    pallas_call x1, Pallas kernels, per_device(): pl.pallas_call(functools.partial(aggregate_kernel, slots), grid=(steps,),...  3.97 us
    pallas_call x1, Pallas kernels, per_device(): pl.pallas_call(functools.partial(dense_kernel, min(part, 256)), out_shape...  2.34 us
    pallas_call x1, Pallas kernels, per_device(): pl.pallas_call(functools.partial(finish_kernel, slots), out_shape=shape((...  2.19 us

profile of v3, /device:TPU:0, one launch (start us, length us, event | category | flops | bytes accessed | tf_op | source)
XLA Modules:
  0.0 80.0 jit_solution(5457506303487905215)
XLA Ops:
  0.6 0.0 copy-start.7
  0.6 0.0 copy-start.6
  0.7 0.8 copy.17.send_ref
  1.4 0.8 %copy.16.bias_ref = f32[256,1]{1,0:T(8,128)S(1)} copy(f32[256,1]{0,1:T(1,128)} %bitcast.15) | data formatting | bytes 2048 | tf_op jit(solution)/shard_map/reshape | solution.py:460
  2.2 0.0 copy-start
  2.2 1.0 %copy-done = bf16[128,2048]{1,0:T(8,128)(2,1)S(1)} copy-done((bf16[128,2048]{1,0:T(8,128)(2,1)S(1)}, bf16[128,2048]{1,0:T(8,128)(2,1)}, u32[]{:S(2)}) %copy-start) | copy-done | bytes 524312
  3.3 0.9 %pack.1.sbuf = bf16[8,128,512]{2,1,0:T(8,128)(2,1)S(1)} custom-call(s32[1,8,4]{2,1,0:T(8,128)S(1)} %copy.17.send_ref, bf16[128,2048]{1,0:T(8,128)(2,1)S(1)} %copy-done), custom_call_target="tpu_custom_call" | custom-call | tf_op jit(solution)/shard_map/pack/pallas_call | solution.py:397
  4.2 0.0 copy-start.1
  4.2 1.0 %copy-done.1 = bf16[128,2048]{1,0:T(8,128)(2,1)S(1)} copy-done((bf16[128,2048]{1,0:T(8,128)(2,1)S(1)}, bf16[128,2048]{1,0:T(8,128)(2,1)}, u32[]{:S(2)}) %copy-start.1) | copy-done | bytes 524312
  5.2 0.0 copy-start.3
  5.2 1.0 %copy-done.3 = bf16[128,2048]{1,0:T(8,128)(2,1)S(1)} copy-done((bf16[128,2048]{1,0:T(8,128)(2,1)S(1)}, bf16[128,2048]{1,0:T(8,128)(2,1)}, u32[]{:S(2)}) %copy-start.3) | copy-done | bytes 524312
  6.2 0.0 copy-start.4
  6.3 0.0 copy-start.5
  6.3 20.8 %halo.1 = (bf16[8,128,512]{2,1,0:T(8,128)(2,1)S(1)}, bf16[2,128,1024]{2,1,0:T(8,128)(2,1)S(1)}, bf16[2,128,1024]{2,1,0:T(8,128)(2,1)S(1)}) custom-call(bf16[8,128,512]{2,1,0:T(8,128)(2,1)S(1)} %pack.1.sbuf, bf16[128,2048]{1,0:T(8,128)(2,1)S(1)} %copy-done.1, bf16[128,2048]{1,0:T(8,128)(2,1)S(1)} %copy-done.3), custom_call_target="tpu_custom_call" | custom-call | tf_op jit(solution)/shard_map/halo/pallas_call | solution.py:405
  27.1 0.0 copy-done.7
  27.1 0.0 copy-done.6
  27.1 0.0 copy-start.2
  27.1 2.0 %copy-done.2 = s32[56,128,128]{2,1,0:T(8,128)S(1)} copy-done((s32[56,128,128]{2,1,0:T(8,128)S(1)}, s32[56,128,128]{2,1,0:T(8,128)}, u32[]{:S(2)}) %copy-start.2) | copy-done | bytes 3670040
  29.2 4.0 %aggregate.1 = (bf16[2,128,1024]{2,1,0:T(8,128)(2,1)S(1)}, f32[2,1,1024]{2,1,0:T(1,128)S(1)}, bf16[56,128,128]{2,1,0:T(8,128)(2,1)S(1)}, s32[32]{0:T(128)S(1)}) custom-call(s32[56]{0:T(128)S(1)} %copy-done.6, s32[56]{0:T(128)S(1)} %copy-done.7, bf16[128,2048]{1,0:T(8,128)(2,1)S(1)} %copy-done.1, bf16[8,128,512]{2,1,0:T(8,128)(2,1)S(1)} %get-tuple-element.21.recv_ref, ...), custom_call_target="tpu_custom_call" | custom-call | tf_op jit(solution)/shard_map/aggregate/pallas_call | solution.py:420
  33.1 7.9 %swap_aggregate.1 = bf16[2,128,1024]{2,1,0:T(8,128)(2,1)S(1)} custom-call(bf16[2,128,1024]{2,1,0:T(8,128)(2,1)S(1)} %get-tuple-element.25.src_ref), custom_call_target="tpu_custom_call" | custom-call | tf_op jit(solution)/shard_map/swap_aggregate/pallas_call | solution.py:435
  41.1 0.0 copy-done.4
  41.1 0.0 copy-done.5
  41.1 2.3 %dense.1 = (bf16[2,8,64,128]{3,2,1,0:T(8,128)(2,1)S(1)}, bf16[2,8,64,128]{3,2,1,0:T(8,128)(2,1)S(1)}, bf16[2,128,1024]{2,1,0:T(8,128)(2,1)S(1)}, bf16[2,256,384]{2,1,0:T(8,128)(2,1)S(1)}) custom-call(bf16[256,1024]{1,0:T(8,128)(2,1)S(1)} %bitcast.9, bf16[256,1024]{1,0:T(8,128)(2,1)S(1)} %bitcast.8, bf16[256,1024]{1,0:T(8,128)(2,1)S(1)} %bitcast.10, ...), custom_call_target="tpu_custom_call" | custom-call | tf_op jit(solution)/shard_map/dense/pallas_call | solution.py:450
  43.4 33.2 %give_back.1 = (bf16[16,64,128]{2,1,0:T(8,128)(2,1)S(1)}, bf16[16,64,128]{2,1,0:T(8,128)(2,1)S(1)}, bf16[2,32,64,128]{3,2,1,0:T(8,128)(2,1)S(1)}, bf16[2,128,102...) custom-call(s32[32]{0:T(128)S(1)} %get-tuple-element.23.slot_dst, ...), custom_call_target="tpu_custom_call" | custom-call | tf_op jit(solution)/shard_map/give_back/pallas_call | solution.py:467
  76.6 2.2 %finish.1 = bf16[128,2048]{1,0:T(8,128)(2,1)} custom-call(s32[1,8,4]{2,1,0:T(8,128)S(1)} %copy.17.send_ref, s32[56]{0:T(128)S(1)} %copy-done.6, s32[56]{0:T(128)S(1)} %copy-done.7, bf16[56,128,128]{2,1,0:T(8,128)(2,1)S(1)} %get-tuple-element.22.half_ref, bf16[16,64,128]{2,1,0:T(8,128)(2,1)S(1)} %get-tuple-element.32.all_a, ...), custom_call_target="tpu_custom_call" | custom-call | tf_op jit(solution)/shard_map/finish/pallas_call | solution.py:491
  78.8 0.7 fusion
  79.5 0.5 copy.19
Async XLA Ops:
  0.6 26.5 %copy-start.7 = (s32[56]{0:T(128)S(1)}, s32[56]{0:T(128)}, u32[]{:S(2)}) copy-start(s32[56]{0:T(128)} %src_ref.3) | copy-start | bytes 676
  0.6 26.5 %copy-start.6 = (s32[56]{0:T(128)S(1)}, s32[56]{0:T(128)}, u32[]{:S(2)}) copy-start(s32[56]{0:T(128)} %dst_ref.3) | copy-start | bytes 676
  2.2 1.0 %copy-start = (bf16[128,2048]{1,0:T(8,128)(2,1)S(1)}, bf16[128,2048]{1,0:T(8,128)(2,1)}, u32[]{:S(2)}) copy-start(bf16[128,2048]{1,0:T(8,128)(2,1)} %feat_ref.5) | copy-start | bytes 1572868
  4.2 1.0 %copy-start.1 = (bf16[128,2048]{1,0:T(8,128)(2,1)S(1)}, bf16[128,2048]{1,0:T(8,128)(2,1)}, u32[]{:S(2)}) copy-start(bf16[128,2048]{1,0:T(8,128)(2,1)} %feat_ref.5) | copy-start | bytes 1572868
  5.2 1.0 %copy-start.3 = (bf16[128,2048]{1,0:T(8,128)(2,1)S(1)}, bf16[128,2048]{1,0:T(8,128)(2,1)}, u32[]{:S(2)}) copy-start(bf16[128,2048]{1,0:T(8,128)(2,1)} %cot_ref.1) | copy-start | bytes 1572868
  6.2 34.8 %copy-start.4 = (bf16[256,256]{1,0:T(8,128)(2,1)S(1)}, bf16[256,256]{1,0:T(8,128)(2,1)}, u32[]{:S(2)}) copy-start(bf16[256,256]{1,0:T(8,128)(2,1)} %ws_ref.1) | copy-start | bytes 393220
  6.3 34.8 %copy-start.5 = (bf16[256,256]{1,0:T(8,128)(2,1)S(1)}, bf16[256,256]{1,0:T(8,128)(2,1)}, u32[]{:S(2)}) copy-start(bf16[256,256]{1,0:T(8,128)(2,1)} %wn_ref.1) | copy-start | bytes 393220
  27.1 2.0 %copy-start.2 = (s32[56,128,128]{2,1,0:T(8,128)S(1)}, s32[56,128,128]{2,1,0:T(8,128)}, u32[]{:S(2)}) copy-start(s32[56,128,128]{2,1,0:T(8,128)} %cnt_ref.1) | copy-start | bytes 11010052

commit v4 on v3

--- a/solution.py
+++ b/solution.py
@@ -9,7 +9,6 @@
 
 MESH = pl.DeviceIdType.MESH
 VMEM_BYTES = 40 * 1024 * 1024
-STEP_TILES = 8
 
 
 def gelu_slope(pre_act):
@@ -36,11 +35,11 @@
     return pl.BlockSpec(memory_space=pl.ANY)
 
 
-def params(collective=None):
+def params(collective=None, vmem_bytes=VMEM_BYTES):
     if collective is None:
-        return pltpu.CompilerParams(vmem_limit_bytes=VMEM_BYTES)
+        return pltpu.CompilerParams(vmem_limit_bytes=vmem_bytes)
     return pltpu.CompilerParams(
-        vmem_limit_bytes=VMEM_BYTES, collective_id=collective, has_side_effects=True
+        vmem_limit_bytes=vmem_bytes, collective_id=collective, has_side_effects=True
     )
 
 
@@ -80,110 +79,145 @@
     ]
 
 
-def pack_kernel(send_ref, feat_ref, out_ref):
-    num_hops, _, width = out_ref.shape
+def pack_kernel(
+    send_ref, dst_ref, src_ref, feat_ref, out_ref, local_ref, tile_of, prev_ref, last_ref, slot_dst
+):
+    slots, piece, side = out_ref.shape[1:]
     cap = send_ref.shape[2]
-    side = width // cap
-    for index in range(num_hops):
-        for slot in range(cap):
-            start = pl.multiple_of(send_ref[0, index, slot] * side, side)
-            out_ref[index, :, slot * side : (slot + 1) * side] = feat_ref[:, pl.ds(start, side)]
-
-
-def halo_kernel(
-    num_blk, num_col, sbuf, feat_ref, cot_ref, recv_ref, feat_all, cot_all,
-    halo_send, halo_recv, col_send, col_recv, own_sem,
+    blocks = last_ref.shape[0]
+    locals_ = local_ref.shape[0]
+    for slot in range(slots):
+        start = pl.multiple_of(send_ref[0, slot // cap, slot % cap] * side, side)
+        picked = feat_ref[:, pl.ds(start, side)]
+        out_ref[0, slot] = picked[:piece]
+        out_ref[1, slot] = picked[piece:]
+    for at in range(locals_):
+        start = pl.multiple_of(src_ref[slots + at] * side, side)
+        local_ref[at] = feat_ref[:, pl.ds(start, side)]
+    for block in range(blocks):
+        last_ref[block] = 0
+
+    def link(at, dst):
+        prev_ref[at] = last_ref[dst]
+        last_ref[dst] = at + 1
+
+    def local_step(at, carry):
+        link(at, dst_ref[slots + at])
+        return carry
+
+    def find_step(tile, carry):
+        tile_of[src_ref[tile] - blocks] = tile
+        return carry
+
+    def slot_step(slot, carry):
+        dst = dst_ref[tile_of[slot]]
+        slot_dst[slot] = dst
+        link(locals_ + slot, dst)
+        return carry
+
+    lax.fori_loop(0, locals_, local_step, 0)
+    lax.fori_loop(0, slots, find_step, 0)
+    lax.fori_loop(0, slots, slot_step, 0)
+
+
+def gather_kernel(
+    num_blk, num_col, tile_of, prev_ref, last_ref, sbuf, local_ref, feat_ref, cot_ref, cnt_hbm,
+    feat_all, cot_all, all_a, all_b, floor_ref, half_ref,
+    recv, sum_a, sum_b, sum_d, agg_src, cnt_ref,
+    halo_send, halo_recv, col_send, col_recv, own_sem, cnt_sem,
 ):
-    num_hops = sbuf.shape[0]
+    slots, piece, side = sbuf.shape[1:]
+    num_hops = halo_send.shape[1]
+    cap = slots // num_hops
     part = feat_all.shape[2]
+    dim = 2 * piece
+    locals_ = local_ref.shape[0]
+    blocks = last_ref.shape[0]
+    per_part = part // side
     row, col, col_peer = positions(num_blk, num_col)
     halo = halo_peers(row, col, num_blk, num_hops, 1)
+    counts_in = pltpu.make_async_copy(cnt_hbm, cnt_ref, cnt_sem)
+    counts_in.start()
     greet(halo + col_peer)
-    copies = []
-    for index in range(num_hops):
-        copies.append(
-            push(sbuf.at[index], recv_ref.at[index], halo_send.at[index], halo_recv.at[index], halo[index])
-        )
-    mine = pl.ds(pl.multiple_of(col * part, part), part)
-    for at, (source, target) in enumerate(((feat_ref, feat_all), (cot_ref, cot_all))):
-        for step, peer in enumerate(col_peer):
-            theirs = pl.ds(pl.multiple_of(peer[1] * part, part), part)
+    halves = []
+    for index in range(2):
+        copies = []
+        for at in range(num_hops):
+            some = pl.ds(at * cap, cap)
             copies.append(
                 push(
-                    source.at[:, theirs], target.at[col], col_send.at[at, step],
-                    col_recv.at[at, step], peer,
+                    sbuf.at[index, some], recv.at[index, some], halo_send.at[index, at],
+                    halo_recv.at[index, at], halo[at],
                 )
             )
-        own = pltpu.make_async_copy(source.at[:, mine], target.at[col], own_sem.at[at])
+        halves.append(copies)
+    later = []
+
+    def share(at, pick, target):
+        for step, peer in enumerate(col_peer):
+            later.append(push(pick(peer[1]), target.at[col], col_send.at[at, step], col_recv.at[at, step], peer))
+        own = pltpu.make_async_copy(pick(col), target.at[col], own_sem.at[at])
         own.start()
-        copies.append(own)
-    for copy in copies:
+        later.append(own)
+
+    def nodes_of(source):
+        return lambda index: source.at[:, pl.ds(pl.multiple_of(index * part, part), part)]
+
+    share(0, nodes_of(feat_ref), feat_all)
+    share(1, nodes_of(cot_ref), cot_all)
+    ones = jnp.ones((16, side), jnp.bfloat16)
+    for total in (sum_a, sum_b, sum_d):
+        total[0] = jnp.zeros(total.shape[1:], jnp.float32)
+    counts_in.wait()
+
+    def times(left, counts):
+        return lax.dot_general(left, counts, (((1,), (1,)), ((), ())), preferred_element_type=jnp.float32)
+
+    def local_step(at, carry):
+        counts = cnt_ref[slots + at].astype(jnp.float32).astype(jnp.bfloat16)
+        half_ref[slots + at] = counts
+        product = times(jnp.concatenate([local_ref[at], ones], axis=0), counts)
+        before = prev_ref[at]
+        sum_a[at + 1] = sum_a[before] + product[:piece]
+        sum_b[at + 1] = sum_b[before] + product[piece:dim]
+        sum_d[at + 1] = sum_d[before] + product[dim:]
+        return carry
+
+    def first_step(slot, carry):
+        counts = cnt_ref[tile_of[slot]].astype(jnp.float32).astype(jnp.bfloat16)
+        half_ref[slot] = counts
+        product = times(jnp.concatenate([recv[0, slot], ones], axis=0), counts)
+        before = prev_ref[locals_ + slot]
+        sum_a[locals_ + slot + 1] = sum_a[before] + product[:piece]
+        sum_d[locals_ + slot + 1] = sum_d[before] + product[piece:]
+        return carry
+
+    def second_step(slot, carry):
+        before = prev_ref[locals_ + slot]
+        sum_b[locals_ + slot + 1] = sum_b[before] + times(recv[1, slot], half_ref[slot])
+        return carry
+
+    lax.fori_loop(0, locals_, local_step, 0, unroll=4)
+    for index, (step, total, target) in enumerate(
+        ((first_step, sum_a, all_a), (second_step, sum_b, all_b))
+    ):
+        for at, copy in enumerate(halves[index]):
+            copy.wait()
+            lax.fori_loop(at * cap, (at + 1) * cap, step, 0, unroll=True)
+        for block in range(blocks):
+            last = last_ref[block]
+            group, left = block // per_part, (block % per_part) * side
+            floor = jnp.maximum(sum_d[last][0:1], 1.0)
+            if index == 0:
+                floor_ref[group, :, left : left + side] = floor
+            agg_src[index, group, :, left : left + side] = (total[last] / floor).astype(jnp.bfloat16)
+        share(2 + index, lambda where: agg_src.at[index, where], target)
+    for copy in later:
         copy.wait()
 
 
-def aggregate_kernel(slots, dst_ref, src_ref, feat_ref, recv_ref, cnt_ref, agg_ref, floor_ref,
-                     half_ref, slot_dst_ref, acc):
-    step = pl.program_id(0)
-    blocks, rows, side = acc.shape
-    dim = feat_ref.shape[0]
-    num_hops = recv_ref.shape[0]
-    cap = slots // num_hops
-    tiles = cnt_ref.shape[0]
-
-    @pl.when(step == 0)
-    def _():
-        acc[...] = jnp.zeros_like(acc)
-
-    def add(tile, picked, place):
-        counts = cnt_ref[tile].astype(jnp.float32).astype(jnp.bfloat16)
-        half_ref[place] = counts
-        left = jnp.concatenate([picked, jnp.ones((rows - dim, side), jnp.bfloat16)], axis=0)
-        product = lax.dot_general(
-            left, counts, (((1,), (1,)), ((), ())), preferred_element_type=jnp.float32
-        )
-        dst = dst_ref[step * tiles + tile]
-        acc[dst] += product
-
-    @pl.when(step * tiles < slots)
-    def _():
-        for tile in range(tiles):
-            slot = src_ref[step * tiles + tile] - blocks
-            start = pl.multiple_of(lax.rem(slot, cap) * side, side)
-            add(tile, recv_ref[lax.div(slot, cap), :, pl.ds(start, side)], slot)
-            slot_dst_ref[slot] = dst_ref[step * tiles + tile]
-
-    @pl.when(step * tiles >= slots)
-    def _():
-        for tile in range(tiles):
-            start = pl.multiple_of(src_ref[step * tiles + tile] * side, side)
-            add(tile, feat_ref[:, pl.ds(start, side)], step * tiles + tile)
-
-    @pl.when(step == pl.num_programs(0) - 1)
-    def _():
-        per_part = agg_ref.shape[2] // side
-        for block in range(blocks):
-            part, at = block // per_part, (block % per_part) * side
-            floor = jnp.maximum(acc[block, dim : dim + 1, :], 1.0)
-            floor_ref[part, :, at : at + side] = floor
-            agg_ref[part, :, at : at + side] = (acc[block, :dim, :] / floor).astype(jnp.bfloat16)
-
-
-def swap_kernel(num_blk, num_col, src_ref, dst_ref, send_sem, recv_sem, own_sem):
-    row, col, col_peer = positions(num_blk, num_col)
-    greet(col_peer)
-    copies = [
-        push(src_ref.at[peer[1]], dst_ref.at[col], send_sem.at[step], recv_sem.at[step], peer)
-        for step, peer in enumerate(col_peer)
-    ]
-    own = pltpu.make_async_copy(src_ref.at[col], dst_ref.at[col], own_sem)
-    own.start()
-    for copy in copies:
-        copy.wait()
-    own.wait()
-
-
 def dense_kernel(
-    chunk, feat_ref, agg_ref, cot_ref, floor_ref, ws_ref, wn_ref, bias_ref,
+    chunk, feat_ref, agg_a, agg_b, cot_ref, floor_ref, ws_ref, wn_ref, bias_ref,
     *outs,
 ):
     scaled_refs, (self_ref, grad_ref, acc) = outs[:-3], outs[-3:]
@@ -194,10 +228,13 @@
     self_weight, neigh_weight = ws_ref[...], wn_ref[...]
     first = (((0,), (0,)), ((), ()))
     last = (((1,), (1,)), ((), ()))
-    bias = bias_ref[...]
+    bias = jnp.transpose(jnp.broadcast_to(bias_ref[...], (8, width)))[:, 0:1]
     for start in range(0, nodes, chunk):
         at = slice(start, start + chunk)
-        feat, agg = feat_ref[:, at], agg_ref[:, at]
+        feat = feat_ref[:, at]
+        agg = jnp.concatenate(
+            [half[part, :, at] for part in range(parts) for half in (agg_a, agg_b)], axis=0
+        )
         pre_act = (
             lax.dot_general(self_weight, feat, first, preferred_element_type=jnp.float32)
             + lax.dot_general(neigh_weight, agg, first, preferred_element_type=jnp.float32)
@@ -326,7 +363,6 @@
     settle(second)
     owns[1].wait()
     spread(1, all_b)
-    later += give(1)
     settle(ups)
     total = far_src[far].astype(jnp.float32)
     for step in range(far_size - 1):
@@ -340,13 +376,15 @@
         total += side_buf[step].astype(jnp.float32)
     bias_out[...] = total[0:1, width:]
     grad_out[core, mid, far] = total[:, :width].astype(jnp.bfloat16)
-    settle([
+    downs = [
         push(
             grad_out.at[core, mid, far], grad_out.at[core, mid, far], down_send.at[3 + step],
             down_recv.at[3 + step], peer,
         )
         for step, peer in enumerate(far_peers)
-    ])
+    ]
+    later += give(1)
+    settle(downs)
     settle([
         push(grad_out.at[core, mid], grad_out.at[core, mid], down_send.at[at], down_recv.at[at], peer)
         for at, peer in enumerate((core_peer, mid_peer, cross_peer))
@@ -356,11 +394,16 @@
 
 
 def finish_kernel(
-    slots, send_ref, dst_ref, src_ref, half_ref, all_a, all_b, self_ref, came_ref, out_ref, acc
+    slots, send_ref, dst_ref, src_ref, half_ref, all_a, all_b, self_ref, came_ref, grad_ref, bias_ref,
+    out_ref, grad_self, grad_neigh, grad_bias, acc,
 ):
     blocks, _, side = acc.shape
     num_hops, cap = send_ref.shape[1:]
     piece = all_a.shape[1]
+    dim = grad_self.shape[0]
+    grad_self[...] = grad_ref[:dim].astype(jnp.float32)
+    grad_neigh[...] = grad_ref[dim:].astype(jnp.float32)
+    grad_bias[...] = bias_ref[:, :dim]
     acc[...] = jnp.zeros_like(acc)
     for tile in range(slots, dst_ref.shape[0]):
         dst = dst_ref[tile]
@@ -392,72 +435,54 @@
     shape = jax.ShapeDtypeStruct
     peers = max(num_col - 1, 1)
     split = shape((num_col, dim, part), half)
-    slot_shape = shape((num_hops, dim, cap * side), half)
-
-    outgoing = pl.pallas_call(
+    locals_ = tiles - slots
+    piece = dim // 2
+    slot_shape = shape((2, slots, piece, side), half)
+    ints = lambda count: shape((count,), jnp.int32)
+
+    outgoing, local_src, tile_of, prev, last, slot_dst = pl.pallas_call(
         pack_kernel,
-        out_shape=slot_shape,
-        in_specs=[smem(), vmem()],
-        out_specs=vmem(),
+        out_shape=(
+            slot_shape, shape((locals_, dim, side), half), ints(slots), ints(tiles), ints(blocks), ints(slots),
+        ),
+        in_specs=[smem()] * 3 + [vmem()],
+        out_specs=(vmem(), vmem()) + (smem(),) * 4,
         compiler_params=params(),
         name="pack",
-    )(send_blk, node_feats)
-    received, feat_all, cot_all = pl.pallas_call(
-        functools.partial(halo_kernel, num_blk, num_col),
-        out_shape=(slot_shape, split, split),
-        in_specs=[anywhere()] * 3,
-        out_specs=(anywhere(),) * 3,
+    )(send_blk, tile_dst, tile_src, node_feats)
+    agg_shape = shape((num_col, piece, part), half)
+    hbm = pl.BlockSpec(memory_space=pltpu.HBM)
+    sums = lambda count: pltpu.VMEM((tiles + 1, count, side), full)
+    feat_all, cot_all, agg_a, agg_b, floor, half_cnt = pl.pallas_call(
+        functools.partial(gather_kernel, num_blk, num_col),
+        out_shape=(
+            split, split, agg_shape, agg_shape, shape((num_col, 1, part), full), shape((tiles, side, side), half),
+        ),
+        in_specs=[smem()] * 3 + [vmem()] * 2 + [hbm] * 3,
+        out_specs=(vmem(),) * 6,
         scratch_shapes=[
-            dma((num_hops,)), dma((num_hops,)), dma((2, peers)), dma((2, peers)), dma((2,)),
+            pltpu.VMEM(slot_shape.shape, half), sums(piece), sums(piece), sums(16),
+            pltpu.VMEM((2, num_col, piece, part), half), pltpu.VMEM((tiles, side, side), jnp.int32),
+            dma((2, num_hops)), dma((2, num_hops)), dma((4, peers)), dma((4, peers)), dma((4,)), dma(()),
         ],
-        compiler_params=params(0),
-        name="halo",
-    )(outgoing, node_feats, cotangent)
-
-    steps = tiles // STEP_TILES
-    cnt_spec = pl.BlockSpec((STEP_TILES, side, side), lambda step: (step, 0, 0))
-    whole = lambda dims: pl.BlockSpec(dims, lambda step: (0,) * len(dims))
-    aggregate, floor, half_cnt, slot_dst = pl.pallas_call(
-        functools.partial(aggregate_kernel, slots),
-        grid=(steps,),
-        out_shape=(
-            split, shape((num_col, 1, part), full), shape((tiles, side, side), half),
-            shape((slots,), jnp.int32),
-        ),
-        in_specs=[smem(), smem(), whole((dim, rows)), whole(slot_shape.shape), cnt_spec],
-        out_specs=(whole(split.shape), whole((num_col, 1, part)), whole((tiles, side, side)), smem()),
-        scratch_shapes=[pltpu.VMEM((blocks, dim + 16, side), full)],
-        compiler_params=params(),
-        name="aggregate",
-    )(tile_dst, tile_src, node_feats, received, tile_cnt)
-
-    def swap(array, collective, name):
-        return pl.pallas_call(
-            functools.partial(swap_kernel, num_blk, num_col),
-            out_shape=split,
-            in_specs=[anywhere()],
-            out_specs=anywhere(),
-            scratch_shapes=[dma((peers,)), dma((peers,)), dma(())],
-            compiler_params=params(collective),
-            name=name,
-        )(array)
-
-    agg_all = swap(aggregate, 1, "swap_aggregate")
+        compiler_params=params(0, 56 * 1024 * 1024),
+        name="gather",
+    )(tile_of, prev, last, outgoing, local_src, node_feats, cotangent, tile_cnt)
+
     lanes = width + 128
     per_part = part // side
-    piece = dim // 2
     scaled_shape = shape((num_col, per_part, piece, side), half)
     scaled_a, scaled_b, own_part, grads = pl.pallas_call(
         functools.partial(dense_kernel, min(part, 256)),
         out_shape=(scaled_shape, scaled_shape, split, shape((num_col, 2 * dim, lanes), half)),
-        in_specs=[vmem()] * 7,
+        in_specs=[vmem()] * 8,
         out_specs=(vmem(),) * 4,
         scratch_shapes=[pltpu.VMEM((2 * width + 16, width), full)],
         compiler_params=params(),
         name="dense",
     )(
-        feat_all.reshape(width, part), agg_all.reshape(width, part), cot_all.reshape(width, part),
-        floor, self_weight, neigh_weight, bias.reshape(width, 1),
+        feat_all.reshape(width, part), agg_a, agg_b, cot_all.reshape(width, part),
+        floor, self_weight, neigh_weight, bias.reshape(1, width),
     )
 
     far_size = num_blk // 4
@@ -488,17 +513,20 @@
         grads.reshape(num_col, 2, 2, far_size, span, lanes),
     )
 
-    grad_feats = pl.pallas_call(
+    weight_shape = shape((dim, width), full)
+    grad_feats, grad_self, grad_neigh, grad_bias = pl.pallas_call(
         functools.partial(finish_kernel, slots),
-        out_shape=shape((dim, rows), half),
-        in_specs=[smem()] * 3 + [vmem()] * 5,
-        out_specs=vmem(),
+        out_shape=(shape((dim, rows), half), weight_shape, weight_shape, shape((1, dim), full)),
+        in_specs=[smem()] * 3 + [vmem()] * 7,
+        out_specs=(vmem(),) * 4,
         scratch_shapes=[pltpu.VMEM((blocks, dim, side), full)],
         compiler_params=params(),
         name="finish",
-    )(send_blk, tile_dst, tile_src, half_cnt, all_a, all_b, own_all, came)
-    grad_both = grad_sum.reshape(2 * dim, width).astype(full)
-    return (grad_feats, grad_both[:dim], grad_both[dim:], bias_sum[0, :dim])
+    )(
+        send_blk, tile_dst, tile_src, half_cnt, all_a, all_b, own_all, came,
+        grad_sum.reshape(2 * dim, width), bias_sum,
+    )
+    return (grad_feats, grad_self, grad_neigh, grad_bias.reshape(dim))
 
 
 def solution(mesh):

time: 80.4 us -> 78.8 us (0.980)
  Pallas kernels: 71.3 us -> 65.8 us
  local copies, waits for them, and re-layouts: 7.98 us -> 11.8 us
    unnamed x18 -> x41, local copies, waits for them, and re-layouts: 6.45 us -> 11.8 us
    pallas_call x1, Pallas kernels: 33.2 us -> 29.3 us  [per_device(): pl.pallas_call(functools.partial(return_kernel, num_blk, num_col), out_sh...]
    pallas_call x5 -> x3, Pallas kernels: 35.8 us -> 34.1 us  [the longest x1 29.3 us: per_device(): pl.pallas_call(functools.partial(gather_kernel, num_blk, num_col), out_sh...]
    reshape x1 -> x0, local copies, waits for them, and re-layouts: 0.8 us -> none  [per_device(): bias.reshape(width, 1)]
where the time goes in v4:
time: 78.8 us; the launch traced here: 78.4 us
  Pallas kernels  65.8 us (84%)
  local copies, waits for them, and re-layouts  11.8 us (15%)
    pallas_call x1, Pallas kernels, per_device(): pl.pallas_call(functools.partial(gather_kernel, num_blk, num_col), out_sh...  29.3 us
    pallas_call x1, Pallas kernels, per_device(): pl.pallas_call(functools.partial(return_kernel, num_blk, num_col), out_sh...  29.3 us
    unnamed x41, local copies, waits for them, and re-layouts  11.8 us
    pallas_call x1, Pallas kernels, per_device(): pl.pallas_call(pack_kernel, out_shape=(slot_shape, shape((locals_, dim, s...  2.56 us
    pallas_call x1, Pallas kernels, per_device(): pl.pallas_call(functools.partial(dense_kernel, min(part, 256)), out_shape...  2.37 us
    pallas_call x1, Pallas kernels, per_device(): pl.pallas_call(functools.partial(finish_kernel, slots), out_shape=(shape(...  2.25 us

profile of v4, /device:TPU:0, one launch (start us, length us, event | category | flops | bytes accessed | tf_op | source)
XLA Modules:
  0.0 78.4 jit_solution(8057361621258315930)
XLA Ops:
  0.6 0.0 copy-start.16
  0.6 0.8 copy.14.send_ref
  1.4 0.0 copy-start.2
  1.4 1.0 %copy-done.2 = bf16[128,2048]{1,0:T(8,128)(2,1)S(1)} copy-done((bf16[128,2048]{1,0:T(8,128)(2,1)S(1)}, bf16[128,2048]{1,0:T(8,128)(2,1)}, u32[]{:S(2)}) %copy-start.2) | copy-done | bytes 524312
  2.4 0.0 copy-start.12
  2.4 0.7 copy-done.12
  3.1 0.0 copy-start.14
  3.1 0.7 copy-done.14
  3.8 0.0 copy-start.9
  3.8 0.0 copy-start.10
  3.8 2.6 %pack.1 = (bf16[2,32,64,128]{3,2,1,0:T(8,128)(2,1)S(1)}, bf16[24,128,128]{2,1,0:T(8,128)(2,1)S(1)}, s32[32]{0:T(128)S(1)}, s32[56]{0:T(128)S(1)}, s32[16]{0:T(128)S(1)}, /*index=5*/s32[32]{0:T(128)S(1)}) custom-call(s32[1,8,4]{2,1,0:T(8,128)S(1)} %copy.14.send_ref, s32[56]{0:T(128)S(1)} %copy-done.12, s32[56]{0:T(128)S(1)} %copy-done.14, ...), custom_call_target="tpu_custom_call" | custom-call | tf_op jit(solution)/shard_map/pack/pallas_call | solution.py:443
  6.3 0.0 copy-start.3
  6.3 1.0 %copy-done.3 = bf16[2,32,64,128]{3,2,1,0:T(8,128)(2,1)} copy-done((bf16[2,32,64,128]{3,2,1,0:T(8,128)(2,1)}, bf16[2,32,64,128]{3,2,1,0:T(8,128)(2,1)S(1)}, u32[]{:S(2)}) %copy-start.3) | copy-done | bytes 1048600
  7.3 0.0 copy-start.4
  7.3 0.9 %copy-done.4 = bf16[24,128,128]{2,1,0:T(8,128)(2,1)} copy-done((bf16[24,128,128]{2,1,0:T(8,128)(2,1)}, bf16[24,128,128]{2,1,0:T(8,128)(2,1)S(1)}, u32[]{:S(2)}) %copy-start.4) | copy-done | bytes 786456
  8.2 0.0 copy-start.17
  8.2 0.0 copy-start.18
  8.2 0.0 copy-start.19
  8.2 0.5 copy-done.17
  8.7 0.0 copy-done.18
  8.7 0.0 copy-done.19
  8.7 0.0 copy-start.13
  8.7 0.0 copy-start.15
  8.7 29.3 %gather.1 = (bf16[2,128,1024]{2,1,0:T(8,128)(2,1)}, bf16[2,128,1024]{2,1,0:T(8,128)(2,1)}, bf16[2,64,1024]{2,1,0:T(8,128)(2,1)}, bf16[2,64,1024]{2,1,0:T(8,128)(...) custom-call(s32[32]{0:T(128)} %copy-done.17, s32[56]{0:T(128)} %copy-done.18, s32[16]{0:T(128)} %copy-done.19, ...), custom_call_target="tpu_custom_call" | custom-call | tf_op jit(solution)/shard_map/gather/pallas_call | solution.py:456
  38.1 0.0 copy-start.1
  38.1 0.0 copy-done.16
  38.1 0.0 copy-done.9
  38.1 0.0 copy-done.10
  38.1 0.0 copy-start.5
  38.1 1.2 %copy-done.5 = bf16[2,128,1024]{2,1,0:T(8,128)(2,1)S(1)} copy-done((bf16[2,128,1024]{2,1,0:T(8,128)(2,1)S(1)}, bf16[2,128,1024]{2,1,0:T(8,128)(2,1)}, u32[]{:S(2)}) %copy-start.5) | copy-done | bytes 524312
  39.3 0.0 copy-start.6
  39.3 1.0 %copy-done.6 = bf16[2,128,1024]{2,1,0:T(8,128)(2,1)S(1)} copy-done((bf16[2,128,1024]{2,1,0:T(8,128)(2,1)S(1)}, bf16[2,128,1024]{2,1,0:T(8,128)(2,1)}, u32[]{:S(2)}) %copy-start.6) | copy-done | bytes 524312
  40.3 0.0 copy-start.7
  40.3 0.9 %copy-done.7 = bf16[2,64,1024]{2,1,0:T(8,128)(2,1)S(1)} copy-done((bf16[2,64,1024]{2,1,0:T(8,128)(2,1)S(1)}, bf16[2,64,1024]{2,1,0:T(8,128)(2,1)}, u32[]{:S(2)}) %copy-start.7) | copy-done | bytes 262168
  41.3 0.0 copy-start.8
  41.3 0.9 %copy-done.8 = bf16[2,64,1024]{2,1,0:T(8,128)(2,1)S(1)} copy-done((bf16[2,64,1024]{2,1,0:T(8,128)(2,1)S(1)}, bf16[2,64,1024]{2,1,0:T(8,128)(2,1)}, u32[]{:S(2)}) %copy-start.8) | copy-done | bytes 262168
  42.2 0.0 copy-start.11
  42.2 0.7 copy-done.11
  42.9 2.4 %dense.1 = (bf16[2,8,64,128]{3,2,1,0:T(8,128)(2,1)S(1)}, bf16[2,8,64,128]{3,2,1,0:T(8,128)(2,1)S(1)}, bf16[2,128,1024]{2,1,0:T(8,128)(2,1)S(1)}, bf16[2,256,384]{2,1,0:T(8,128)(2,1)S(1)}) custom-call(bf16[256,1024]{1,0:T(8,128)(2,1)S(1)} %bitcast.6, bf16[2,64,1024]{2,1,0:T(8,128)(2,1)S(1)} %copy-done.7, bf16[2,64,1024]{2,1,0:T(8,128)(2,1)S(1)} %copy-done.8, ...), custom_call_target="tpu_custom_call" | custom-call | tf_op jit(solution)/shard_map/dense/pallas_call | solution.py:475
  45.3 0.0 copy-start
  45.3 1.5 %copy-done = bf16[56,128,128]{2,1,0:T(8,128)(2,1)S(1)} copy-done((bf16[56,128,128]{2,1,0:T(8,128)(2,1)S(1)}, bf16[56,128,128]{2,1,0:T(8,128)(2,1)}, u32[]{:S(2)}) %copy-start) | copy-done | bytes 1835032
  46.8 29.3 %give_back.1 = (bf16[16,64,128]{2,1,0:T(8,128)(2,1)S(1)}, bf16[16,64,128]{2,1,0:T(8,128)(2,1)S(1)}, bf16[2,32,64,128]{3,2,1,0:T(8,128)(2,1)S(1)}, bf16[2,128,102...) custom-call(s32[32]{0:T(128)S(1)} %get-tuple-element.36.slot_dst, ...), custom_call_target="tpu_custom_call" | custom-call | tf_op jit(solution)/shard_map/give_back/pallas_call | solution.py:492
  76.1 0.0 copy-done.13
  76.1 0.0 copy-done.15
  76.1 0.0 copy-done.1
  76.1 2.3 %finish.1 = (bf16[128,2048]{1,0:T(8,128)(2,1)}, f32[128,256]{1,0:T(8,128)}, f32[128,256]{1,0:T(8,128)}, f32[1,128]{1,0:T(1,128)}) custom-call(s32[1,8,4]{2,1,0:T(8,128)S(1)} %copy.14.send_ref, s32[56]{0:T(128)S(1)} %copy-done.13, s32[56]{0:T(128)S(1)} %copy-done.15, bf16[56,128,128]{2,1,0:T(8,128)(2,1)S(1)} %copy-done.1, ...), custom_call_target="tpu_custom_call" | custom-call | tf_op jit(solution)/shard_map/finish/pallas_call | solution.py:517
Async XLA Ops:
  0.6 37.5 %copy-start.16 = (f32[256]{0:T(256)S(1)}, f32[256]{0:T(256)}, u32[]{:S(2)}) copy-start(f32[256]{0:T(256)} %param.16) | copy-start | bytes 3076
  1.4 1.0 %copy-start.2 = (bf16[128,2048]{1,0:T(8,128)(2,1)S(1)}, bf16[128,2048]{1,0:T(8,128)(2,1)}, u32[]{:S(2)}) copy-start(bf16[128,2048]{1,0:T(8,128)(2,1)} %feat_ref.3) | copy-start | bytes 1572868
  2.4 0.7 copy-start.12
  3.1 0.7 copy-start.14
  3.8 34.3 %copy-start.9 = (bf16[256,256]{1,0:T(8,128)(2,1)S(1)}, bf16[256,256]{1,0:T(8,128)(2,1)}, u32[]{:S(2)}) copy-start(bf16[256,256]{1,0:T(8,128)(2,1)} %ws_ref.1) | copy-start | bytes 393220
  3.8 34.3 %copy-start.10 = (bf16[256,256]{1,0:T(8,128)(2,1)S(1)}, bf16[256,256]{1,0:T(8,128)(2,1)}, u32[]{:S(2)}) copy-start(bf16[256,256]{1,0:T(8,128)(2,1)} %wn_ref.1) | copy-start | bytes 393220
  6.3 1.0 %copy-start.3 = (bf16[2,32,64,128]{3,2,1,0:T(8,128)(2,1)}, bf16[2,32,64,128]{3,2,1,0:T(8,128)(2,1)S(1)}, u32[]{:S(2)}) copy-start(bf16[2,32,64,128]{3,2,1,0:T(8,128)(2,1)S(1)} %get-tuple-element.33.sbuf) | copy-start | bytes 3145732
  7.3 0.9 %copy-start.4 = (bf16[24,128,128]{2,1,0:T(8,128)(2,1)}, bf16[24,128,128]{2,1,0:T(8,128)(2,1)S(1)}, u32[]{:S(2)}) copy-start(bf16[24,128,128]{2,1,0:T(8,128)(2,1)S(1)} %get-tuple-element.34.local_ref) | copy-start | bytes 2359300
  8.2 0.5 copy-start.17
  8.2 0.5 copy-start.18
  8.2 0.5 copy-start.19
  8.7 67.4 %copy-start.13 = (s32[56]{0:T(128)S(1)}, s32[56]{0:T(128)}, u32[]{:S(2)}) copy-start(s32[56]{0:T(128)} %dst_ref.3) | copy-start | bytes 676
  8.7 67.4 %copy-start.15 = (s32[56]{0:T(128)S(1)}, s32[56]{0:T(128)}, u32[]{:S(2)}) copy-start(s32[56]{0:T(128)} %src_ref.3) | copy-start | bytes 676
  38.1 38.1 %copy-start.1 = (bf16[56,128,128]{2,1,0:T(8,128)(2,1)S(1)}, bf16[56,128,128]{2,1,0:T(8,128)(2,1)}, u32[]{:S(2)}) copy-start(bf16[56,128,128]{2,1,0:T(8,128)(2,1)} %get-tuple-element.35.half_ref) | copy-start | bytes 5505028
  38.1 1.2 %copy-start.5 = (bf16[2,128,1024]{2,1,0:T(8,128)(2,1)S(1)}, bf16[2,128,1024]{2,1,0:T(8,128)(2,1)}, u32[]{:S(2)}) copy-start(bf16[2,128,1024]{2,1,0:T(8,128)(2,1)} %get-tuple-element.37) | copy-start | bytes 1572868
  39.3 1.0 %copy-start.6 = (bf16[2,128,1024]{2,1,0:T(8,128)(2,1)S(1)}, bf16[2,128,1024]{2,1,0:T(8,128)(2,1)}, u32[]{:S(2)}) copy-start(bf16[2,128,1024]{2,1,0:T(8,128)(2,1)} %get-tuple-element.40) | copy-start | bytes 1572868
  40.3 0.9 %copy-start.7 = (bf16[2,64,1024]{2,1,0:T(8,128)(2,1)S(1)}, bf16[2,64,1024]{2,1,0:T(8,128)(2,1)}, u32[]{:S(2)}) copy-start(bf16[2,64,1024]{2,1,0:T(8,128)(2,1)} %get-tuple-element.38.agg_a) | copy-start | bytes 786436
  41.3 0.9 %copy-start.8 = (bf16[2,64,1024]{2,1,0:T(8,128)(2,1)S(1)}, bf16[2,64,1024]{2,1,0:T(8,128)(2,1)}, u32[]{:S(2)}) copy-start(bf16[2,64,1024]{2,1,0:T(8,128)(2,1)} %get-tuple-element.39.agg_b) | copy-start | bytes 786436
  42.2 0.7 copy-start.11
  45.3 1.5 %copy-start = (bf16[56,128,128]{2,1,0:T(8,128)(2,1)S(1)}, bf16[56,128,128]{2,1,0:T(8,128)(2,1)}, u32[]{:S(2)}) copy-start(bf16[56,128,128]{2,1,0:T(8,128)(2,1)} %get-tuple-element.35.half_ref) | copy-start | bytes 5505028

commit v5 on v4

--- a/solution.py
+++ b/solution.py
@@ -465,7 +465,7 @@
             pltpu.VMEM((2, num_col, piece, part), half), pltpu.VMEM((tiles, side, side), jnp.int32),
             dma((2, num_hops)), dma((2, num_hops)), dma((4, peers)), dma((4, peers)), dma((4,)), dma(()),
         ],
-        compiler_params=params(0, 56 * 1024 * 1024),
+        compiler_params=params(0, 24 * 1024 * 1024),
         name="gather",
     )(tile_of, prev, last, outgoing, local_src, node_feats, cotangent, tile_cnt)
 

time: 78.8 us -> 70.7 us (0.90)
  local copies, waits for them, and re-layouts: 11.8 us -> 6.21 us
  Pallas kernels: 65.8 us -> 63.4 us
    unnamed x41 -> x21, local copies, waits for them, and re-layouts: 11.8 us -> 6.21 us
    pallas_call x1, Pallas kernels: 29.3 us -> 26.9 us  [per_device(): pl.pallas_call(functools.partial(gather_kernel, num_blk, num_col), out_sh...]
where the time goes in v5:
time: 70.7 us; the launch traced here: 70.4 us
  Pallas kernels  63.4 us (90%)
  local copies, waits for them, and re-layouts  6.21 us (9%)
  between operations  0.74 us (1%)
    pallas_call x1, Pallas kernels, per_device(): pl.pallas_call(functools.partial(return_kernel, num_blk, num_col), out_sh...  29.3 us
    pallas_call x1, Pallas kernels, per_device(): pl.pallas_call(functools.partial(gather_kernel, num_blk, num_col), out_sh...  26.9 us
    unnamed x21, local copies, waits for them, and re-layouts  6.21 us
    pallas_call x1, Pallas kernels, per_device(): pl.pallas_call(pack_kernel, out_shape=(slot_shape, shape((locals_, dim, s...  2.56 us
    pallas_call x1, Pallas kernels, per_device(): pl.pallas_call(functools.partial(dense_kernel, min(part, 256)), out_shape...  2.38 us
    pallas_call x1, Pallas kernels, per_device(): pl.pallas_call(functools.partial(finish_kernel, slots), out_shape=(shape(...  2.25 us

profile of v5, /device:TPU:0, one launch (start us, length us, event | category | flops | bytes accessed | tf_op | source)
XLA Modules:
  0.0 70.4 jit_solution(11711006301795975130)
XLA Ops:
  0.6 0.0 copy-start.9
  0.6 0.8 %copy.14.send_ref = s32[1,8,4]{2,1,0:T(8,128)S(1)} copy(s32[1,8,4]{1,2,0:T(4,128)} %param.13) | data formatting | bytes 256 | tf_op args[4]
  1.4 0.0 copy-start.1
  1.4 1.0 %copy-done.1 = bf16[128,2048]{1,0:T(8,128)(2,1)S(1)} copy-done((bf16[128,2048]{1,0:T(8,128)(2,1)S(1)}, bf16[128,2048]{1,0:T(8,128)(2,1)}, u32[]{:S(2)}) %copy-start.1) | copy-done | bytes 524312
  2.4 0.0 copy-start.5
  2.4 0.7 copy-done.5
  3.1 0.0 copy-start.7
  3.1 0.7 copy-done.7
  3.8 0.0 copy-start.3
  3.8 0.0 copy-start.4
  3.8 2.6 %pack.1 = (bf16[2,32,64,128]{3,2,1,0:T(8,128)(2,1)S(1)}, bf16[24,128,128]{2,1,0:T(8,128)(2,1)S(1)}, s32[32]{0:T(128)S(1)}, s32[56]{0:T(128)S(1)}, s32[16]{0:T(128)S(1)}, /*index=5*/s32[32]{0:T(128)S(1)}) custom-call(s32[1,8,4]{2,1,0:T(8,128)S(1)} %copy.14.send_ref, s32[56]{0:T(128)S(1)} %copy-done.5, s32[56]{0:T(128)S(1)} %copy-done.7, ...), custom_call_target="tpu_custom_call" | custom-call | tf_op jit(solution)/shard_map/pack/pallas_call | solution.py:443
  6.3 0.0 copy-start
  6.3 2.0 %copy-done = s32[56,128,128]{2,1,0:T(8,128)S(1)} copy-done((s32[56,128,128]{2,1,0:T(8,128)S(1)}, s32[56,128,128]{2,1,0:T(8,128)}, u32[]{:S(2)}) %copy-start) | copy-done | bytes 3670040
  8.4 0.0 copy-start.2
  8.4 1.0 %copy-done.2 = bf16[128,2048]{1,0:T(8,128)(2,1)S(1)} copy-done((bf16[128,2048]{1,0:T(8,128)(2,1)S(1)}, bf16[128,2048]{1,0:T(8,128)(2,1)}, u32[]{:S(2)}) %copy-start.2) | copy-done | bytes 524312
  9.4 26.9 %gather.1 = (bf16[2,128,1024]{2,1,0:T(8,128)(2,1)S(1)}, bf16[2,128,1024]{2,1,0:T(8,128)(2,1)S(1)}, bf16[2,64,1024]{2,1,0:T(8,128)(2,1)S(1)}, bf16[2,64,1024]{2,1...) custom-call(s32[32]{0:T(128)S(1)} %get-tuple-element.30.tile_of, ...), custom_call_target="tpu_custom_call" | custom-call | tf_op jit(solution)/shard_map/gather/pallas_call | solution.py:456
  36.3 0.0 copy-start.6
  36.3 0.0 copy-start.8
  36.3 0.0 copy-done.9
  36.3 0.0 copy-done.3
  36.3 0.0 copy-done.4
  36.4 2.4 %dense.1 = (bf16[2,8,64,128]{3,2,1,0:T(8,128)(2,1)S(1)}, bf16[2,8,64,128]{3,2,1,0:T(8,128)(2,1)S(1)}, bf16[2,128,1024]{2,1,0:T(8,128)(2,1)S(1)}, bf16[2,256,384]{2,1,0:T(8,128)(2,1)S(1)}) custom-call(bf16[256,1024]{1,0:T(8,128)(2,1)S(1)} %bitcast.6, bf16[2,64,1024]{2,1,0:T(8,128)(2,1)S(1)} %get-tuple-element.38.agg_a, ...), custom_call_target="tpu_custom_call" | custom-call | tf_op jit(solution)/shard_map/dense/pallas_call | solution.py:475
  38.8 29.3 %give_back.1 = (bf16[16,64,128]{2,1,0:T(8,128)(2,1)S(1)}, bf16[16,64,128]{2,1,0:T(8,128)(2,1)S(1)}, bf16[2,32,64,128]{3,2,1,0:T(8,128)(2,1)S(1)}, bf16[2,128,102...) custom-call(s32[32]{0:T(128)S(1)} %get-tuple-element.36.slot_dst, ...), custom_call_target="tpu_custom_call" | custom-call | tf_op jit(solution)/shard_map/give_back/pallas_call | solution.py:492
  68.1 0.0 copy-done.6
  68.1 0.0 copy-done.8
  68.1 2.3 %finish.1 = (bf16[128,2048]{1,0:T(8,128)(2,1)}, f32[128,256]{1,0:T(8,128)}, f32[128,256]{1,0:T(8,128)}, f32[1,128]{1,0:T(1,128)}) custom-call(s32[1,8,4]{2,1,0:T(8,128)S(1)} %copy.14.send_ref, s32[56]{0:T(128)S(1)} %copy-done.6, s32[56]{0:T(128)S(1)} %copy-done.8, bf16[56,128,128]{2,1,0:T(8,128)(2,1)S(1)} %get-tuple-element.35.half_ref, ...), custom_call_target="tpu_custom_call" | custom-call | tf_op jit(solution)/shard_map/finish/pallas_call | solution.py:517
Async XLA Ops:
  0.6 35.7 %copy-start.9 = (f32[256]{0:T(256)S(1)}, f32[256]{0:T(256)}, u32[]{:S(2)}) copy-start(f32[256]{0:T(256)} %param.16) | copy-start | bytes 3076
  1.4 1.0 %copy-start.1 = (bf16[128,2048]{1,0:T(8,128)(2,1)S(1)}, bf16[128,2048]{1,0:T(8,128)(2,1)}, u32[]{:S(2)}) copy-start(bf16[128,2048]{1,0:T(8,128)(2,1)} %feat_ref.3) | copy-start | bytes 1572868
  2.4 0.7 copy-start.5
  3.1 0.7 copy-start.7
  3.8 32.6 %copy-start.3 = (bf16[256,256]{1,0:T(8,128)(2,1)S(1)}, bf16[256,256]{1,0:T(8,128)(2,1)}, u32[]{:S(2)}) copy-start(bf16[256,256]{1,0:T(8,128)(2,1)} %ws_ref.1) | copy-start | bytes 393220
  3.8 32.6 %copy-start.4 = (bf16[256,256]{1,0:T(8,128)(2,1)S(1)}, bf16[256,256]{1,0:T(8,128)(2,1)}, u32[]{:S(2)}) copy-start(bf16[256,256]{1,0:T(8,128)(2,1)} %wn_ref.1) | copy-start | bytes 393220
  6.3 2.0 %copy-start = (s32[56,128,128]{2,1,0:T(8,128)S(1)}, s32[56,128,128]{2,1,0:T(8,128)}, u32[]{:S(2)}) copy-start(s32[56,128,128]{2,1,0:T(8,128)} %cnt_hbm.1) | copy-start | bytes 11010052
  8.4 1.0 %copy-start.2 = (bf16[128,2048]{1,0:T(8,128)(2,1)S(1)}, bf16[128,2048]{1,0:T(8,128)(2,1)}, u32[]{:S(2)}) copy-start(bf16[128,2048]{1,0:T(8,128)(2,1)} %cot_ref.1) | copy-start | bytes 1572868
  36.3 31.8 %copy-start.6 = (s32[56]{0:T(128)S(1)}, s32[56]{0:T(128)}, u32[]{:S(2)}) copy-start(s32[56]{0:T(128)} %dst_ref.3) | copy-start | bytes 676
  36.3 31.8 %copy-start.8 = (s32[56]{0:T(128)S(1)}, s32[56]{0:T(128)}, u32[]{:S(2)}) copy-start(s32[56]{0:T(128)} %src_ref.3) | copy-start | bytes 676
